TPU v7x, 768 devices: a whole 4x8x12 slice. The times are simulated.
768 devices in a mesh: seq: 96 (over x, z, core), head: 8 (over y).
Axes of the slice: x: 4, y: 8, z: 12, core: 2. Of those that a mesh axis runs over, the one named last changes fastest.
Arguments:
- query: bfloat16 [24576, 2048], P('seq', 'head'), may hold values from -6 to 6
- key: bfloat16 [24576, 2048], P('seq', 'head'), may hold values from -6 to 6
- value: bfloat16 [24576, 2048], P('seq', 'head'), may hold values from -6 to 6
- grad_out: bfloat16 [24576, 2048], P(('seq', 'head')), may hold values from -6 to 6
Outputs:
- grad_query: bfloat16 [24576, 2048], P('seq', 'head')
- grad_key: bfloat16 [24576, 2048], P('seq', 'head')
- grad_value: bfloat16 [24576, 2048], P('seq', 'head')
All inputs are finite; a program needn't handle non-finite values.
Results may differ from a plain program's by a relative error of at most 0.0049.
Values may be sent and summed in bfloat16 or wider, within the bound.
No kernel may reach another device: no remote copies, remote signals or barrier semaphores. Data moves between devices by JAX's collectives and lax.ppermute only.
A program may use at most 64 MiB of HBM per device.

v0:
```python
import math

import jax
import jax.numpy as jnp
from jax import lax
from jax.sharding import PartitionSpec as P

DH = 128


def prefix(array, axis, combine, identity, reverse):
    devices, mine = (lax.axis_size(axis), lax.axis_index(axis))
    everything = lax.all_gather(array, axis)
    start = jnp.broadcast_to(jnp.asarray(identity, array.dtype), array.shape)

    def step(k, before):
        at = devices - 1 - k if reverse else k
        reached = at > mine if reverse else at < mine
        new = combine(before, everything[at])
        return jnp.where(reached, new, before)

    return lax.fori_loop(0, devices, step, start)


def add_states(earlier, later):
    return earlier + later


def local(query, key, value, grad_out):
    local_grad = lax.all_to_all(grad_out, "head", split_axis=1, concat_axis=0, tiled=True)
    tokens_here = query.shape[0]
    heads_here = query.shape[1] // DH

    def by_head(x):
        return x.reshape(tokens_here, heads_here, DH).transpose(1, 0, 2)

    query_rows = by_head(query)
    key_rows = by_head(key)
    value_rows = by_head(value)
    grad_rows = by_head(local_grad)
    scale = 1.0 / math.sqrt(DH * tokens_here * lax.axis_size("seq"))
    kv_state = jnp.einsum("htd,hte->hde", key_rows, value_rows, preferred_element_type=jnp.float32)
    qg_state = jnp.einsum("htd,hte->hde", query_rows, grad_rows, preferred_element_type=jnp.float32)
    zero_state = jnp.zeros_like(kv_state)
    before = prefix(kv_state, "seq", add_states, zero_state, False)
    after = prefix(qg_state, "seq", add_states, zero_state, True)
    before_half = before.astype(jnp.bfloat16)
    after_half = after.astype(jnp.bfloat16)
    rowidx = lax.broadcasted_iota(jnp.int32, (tokens_here, tokens_here), 0)
    colidx = lax.broadcasted_iota(jnp.int32, (tokens_here, tokens_here), 1)
    causal = (rowidx >= colidx)[None, :, :]
    score_go = jnp.einsum("htd,hsd->hts", grad_rows, value_rows, preferred_element_type=jnp.float32)
    score_go = jnp.where(causal, score_go, 0.0).astype(jnp.bfloat16)
    score_qk = jnp.einsum("htd,hsd->hts", query_rows, key_rows, preferred_element_type=jnp.float32)
    score_qk = jnp.where(causal, score_qk, 0.0).astype(jnp.bfloat16)
    dquery = jnp.einsum("hts,hsd->htd", score_go, key_rows, preferred_element_type=jnp.float32)
    dquery = dquery + jnp.einsum(
        "hte,hde->htd", grad_rows, before_half, preferred_element_type=jnp.float32
    )
    dkey = jnp.einsum("hts,htd->hsd", score_go, query_rows, preferred_element_type=jnp.float32)
    dkey = dkey + jnp.einsum(
        "hte,hde->htd", value_rows, after_half, preferred_element_type=jnp.float32
    )
    dvalue = jnp.einsum("hts,hte->hse", score_qk, grad_rows, preferred_element_type=jnp.float32)
    dvalue = dvalue + jnp.einsum(
        "htd,hde->hte", key_rows, after_half, preferred_element_type=jnp.float32
    )

    def by_token(x):
        return (
            (x * scale)
            .astype(jnp.bfloat16)
            .transpose(1, 0, 2)
            .reshape(tokens_here, heads_here * DH)
        )

    return (by_token(dquery), by_token(dkey), by_token(dvalue))


def solution(mesh):
    placed = (P("seq", "head"), P("seq", "head"), P("seq", "head"), P(("seq", "head"), None))
    return jax.shard_map(
        local,
        mesh=mesh,
        in_specs=placed,
        out_specs=(P("seq", "head"), P("seq", "head"), P("seq", "head")),
        check_vma=False,
    )
```

profile of v0, /device:TPU:1, one launch (start us, length us, event | category | flops | bytes accessed | tf_op | source)
XLA Modules:
  0.0 383.2 jit_solution(2769753156338149916)
XLA Ops:
  8.1 1.8 fusion.16
  10.9 15.4 %all_to_all.16 = bf16[32,8,256]{2,0,1:T(8,128)(2,1)S(1)} all-to-all(bf16[32,8,256]{2,0,1:T(8,128)(2,1)S(1)} %bitcast.141), channel_id=1, replica_groups=mesh['seq'=96,'head'=8] {'head'}, dimensions={1} | all-to-all | bytes 262144 | tf_op jit(solution)/shard_map/all_to_all | solution.py:30
  26.3 1.8 fusion.15
  28.4 120.5 %all-gather.5.cloned.1.call-done = f32[192,128,128]{2,1,0:T(8,128)} async-done(((f32[2,128,128]{2,1,0:T(8,128)}), f32[192,128,128]{2,1,0:T(8,128)}) %all-gather.5.cloned.1.call-update) | async-done | bytes 12582928 | tf_op jit(solution)/shard_map/all_gather | solution.py:13
  148.8 93.6 %while.30 = (s32[]{:T(128)}, f32[2,128,128]{2,1,0:T(8,128)S(1)}, s32[]{:T(128)}, f32[96,2,128,128]{3,2,1,0:T(8,128)}, s32[]{:T(128)}, /*index=5*/s32[]{:T(128)}) while((s32[]{:T(128)}, f32[2,128,128]{2,1,0:T(8,128)S(1)}, s32[]{:T(128)}, f32[96,2,128,128]{3,2,1,0:T(8,128)}, s32[]{:T(128)}, /*index=5*/s32[]{:T(128)}) %tuple.85), condition=%wide.region_1.2_spmd.clone, body=%wide.region_0.1_spmd.clone.sunk | while | flops 98308 | bytes 393317 | solution.py:22
  149.8 0.9 add_select_fusion.4
  150.8 0.9 add_select_fusion.4
  151.8 0.9 add_select_fusion.4
  171.2 1.0 add_select_fusion.4
  175.1 1.0 add_select_fusion.4
  178.0 1.0 add_select_fusion.4
  180.0 1.0 add_select_fusion.4
  181.0 1.0 add_select_fusion.4
  183.9 1.0 add_select_fusion.4
  190.7 1.0 add_select_fusion.4
  192.6 1.0 add_select_fusion.4
  194.6 1.0 add_select_fusion.4
  198.5 1.0 add_select_fusion.4
  222.8 1.0 add_select_fusion.4
  228.7 1.0 add_select_fusion.4
  229.7 1.0 add_select_fusion.4
  230.7 1.0 add_select_fusion.4
  232.6 1.0 add_select_fusion.4
  234.6 1.0 add_select_fusion.4
  235.6 1.0 add_select_fusion.4
  241.5 1.0 add_select_fusion.4
  242.6 1.2 fusion.10
  244.5 32.6 %all-gather.7.cloned.1.call-done = f32[192,128,128]{2,1,0:T(8,128)} async-done(((f32[2,128,128]{2,1,0:T(8,128)}), f32[192,128,128]{2,1,0:T(8,128)}) %all-gather.7.cloned.1.call-update) | async-done | bytes 12582928 | tf_op jit(solution)/shard_map/all_gather | solution.py:13
  277.2 93.8 %while.31 = (s32[]{:T(128)}, f32[2,128,128]{2,1,0:T(8,128)S(1)}, s32[]{:T(128)}, f32[96,2,128,128]{3,2,1,0:T(8,128)}, s32[]{:T(128)}, /*index=5*/s32[]{:T(128)}, s32[]{:T(128)}, s32[]{:T(128)}) while((s32[]{:T(128)}, f32[2,128,128]{2,1,0:T(8,128)S(1)}, s32[]{:T(128)}, f32[96,2,128,128]{3,2,1,0:T(8,128)}, s32[]{:T(128)}, ...), condition=%wide.region_3.4_spmd.clone, body=%wide.region_2.3_spmd.clone.sunk | while | flops 98312 | bytes 393379 | solution.py:22
  371.2 1.1 convolution_bitcast_fusion.2
  372.3 1.1 fusion.11
  374.2 1.3 fusion.12
  (188 shorter events, 167.3 us)
Async XLA Ops:
  7.2 0.9 copy-start
  7.2 141.7 %all-gather.5.cloned.1.call-start = ((), (), s32[]{:S(2)}) async-start(), calls=%async_computation.1 | async-start | bytes 12713984 | tf_op jit(solution)/shard_map/all_gather | solution.py:13
  9.9 267.3 %all-gather.7.cloned.1.call-start = ((), (), s32[]{:S(2)}) async-start(), calls=%async_computation.2 | async-start | bytes 12713984 | tf_op jit(solution)/shard_map/all_gather | solution.py:13
Sparse Core Ops, SparseCore 0:
  12.3 136.5 all-gather.4
  153.1 124.0 all-gather.6
where the time goes:
time: 387 us; the launch traced here: 383 us
  other arithmetic  183 us (47%)
  waiting for transfers between devices  153 us (40%)
  blocking collectives  15.4 us (4%)
  between operations  14.2 us (4%)
  matrix products  8.93 us (2%)
  loops' own time  4.86 us (1%)
  local copies, waits for them, and re-layouts  4.09 us (1%)
    select_n x192, other arithmetic, step(): return jnp.where(reached, new, before)  183 us
    all_gather x2, waiting for transfers between devices, prefix(): everything = lax.all_gather(array, axis)  153 us
    all_to_all x1, blocking collectives, local(): lax.all_to_all(grad_out, 'head', split_axis=1, concat_axis=0, tiled=True)  15.4 us
  transfers between devices with their start and end apart: 2, of which 2 were waited for; matrix products, arithmetic and copies ran while one was open for 25% of the time, Pallas kernels for 0%

commit v1 on v0

--- a/solution.py
+++ b/solution.py
@@ -3,30 +3,15 @@
 import jax
 import jax.numpy as jnp
 from jax import lax
+from jax.sharding import Mesh
 from jax.sharding import PartitionSpec as P
 
 DH = 128
-
-
-def prefix(array, axis, combine, identity, reverse):
-    devices, mine = (lax.axis_size(axis), lax.axis_index(axis))
-    everything = lax.all_gather(array, axis)
-    start = jnp.broadcast_to(jnp.asarray(identity, array.dtype), array.shape)
-
-    def step(k, before):
-        at = devices - 1 - k if reverse else k
-        reached = at > mine if reverse else at < mine
-        new = combine(before, everything[at])
-        return jnp.where(reached, new, before)
-
-    return lax.fori_loop(0, devices, step, start)
-
-
-def add_states(earlier, later):
-    return earlier + later
+X, Z, C = 4, 12, 2
 
 
 def local(query, key, value, grad_out):
+    x, z, c = (lax.axis_index(axis) for axis in ("x", "z", "c"))
     local_grad = lax.all_to_all(grad_out, "head", split_axis=1, concat_axis=0, tiled=True)
     tokens_here = query.shape[0]
     heads_here = query.shape[1] // DH
@@ -38,14 +23,34 @@
     key_rows = by_head(key)
     value_rows = by_head(value)
     grad_rows = by_head(local_grad)
-    scale = 1.0 / math.sqrt(DH * tokens_here * lax.axis_size("seq"))
+    scale = 1.0 / math.sqrt(DH * tokens_here * X * Z * C)
     kv_state = jnp.einsum("htd,hte->hde", key_rows, value_rows, preferred_element_type=jnp.float32)
     qg_state = jnp.einsum("htd,hte->hde", query_rows, grad_rows, preferred_element_type=jnp.float32)
-    zero_state = jnp.zeros_like(kv_state)
-    before = prefix(kv_state, "seq", add_states, zero_state, False)
-    after = prefix(qg_state, "seq", add_states, zero_state, True)
-    before_half = before.astype(jnp.bfloat16)
-    after_half = after.astype(jnp.bfloat16)
+    first = c == 0
+    own = jnp.where(first, kv_state, qg_state)
+    other = jnp.where(first, qg_state, kv_state).astype(jnp.bfloat16)
+
+    def from_other_core(array):
+        both = lax.all_gather(array, "c")
+        return jnp.where(first, both[1], both[0])
+
+    pair = own + from_other_core(other).astype(jnp.float32)
+    along_z = lax.all_gather(pair.astype(jnp.bfloat16), "z").astype(jnp.float32)
+    places = jnp.arange(Z)
+    wanted = jnp.where(first, places < z, places > z)[:, None, None, None]
+    inside = jnp.sum(jnp.where(wanted, along_z, 0.0), axis=0)
+    plane = jnp.sum(along_z, axis=0).astype(jnp.bfloat16)
+    along_x = lax.all_to_all(
+        jnp.broadcast_to(plane[None], (X, *plane.shape)), "x", 0, 0, tiled=True
+    ).astype(jnp.float32)
+    places = jnp.arange(X)
+    wanted = jnp.where(first, places < x, places > x)[:, None, None, None]
+    mine = inside + jnp.sum(jnp.where(wanted, along_x, 0.0), axis=0)
+    sent = from_other_core((mine + own).astype(jnp.bfloat16))
+    mine = mine.astype(jnp.bfloat16)
+    before_half = jnp.where(first, mine, sent)
+    after_half = jnp.where(first, sent, mine)
+
     rowidx = lax.broadcasted_iota(jnp.int32, (tokens_here, tokens_here), 0)
     colidx = lax.broadcasted_iota(jnp.int32, (tokens_here, tokens_here), 1)
     causal = (rowidx >= colidx)[None, :, :]
@@ -78,11 +83,13 @@
 
 
 def solution(mesh):
-    placed = (P("seq", "head"), P("seq", "head"), P("seq", "head"), P(("seq", "head"), None))
+    split = Mesh(mesh.devices.reshape(X, Z, C, -1), ("x", "z", "c", "head"))
+    rows = ("x", "z", "c")
+    placed = (P(rows, "head"),) * 3
     return jax.shard_map(
         local,
-        mesh=mesh,
-        in_specs=placed,
-        out_specs=(P("seq", "head"), P("seq", "head"), P("seq", "head")),
+        mesh=split,
+        in_specs=(*placed, P((*rows, "head"), None)),
+        out_specs=placed,
         check_vma=False,
     )

time: 387 us -> 77 us (0.20)
  other arithmetic: 183 us -> 0.56 us
  waiting for transfers between devices: 153 us -> 11.8 us
  blocking collectives: 15.4 us -> 44.2 us
  between operations: 14.2 us -> 0.8 us
  starting transfers between devices: 0.08 us -> 11.7 us
  matrix products: 8.93 us -> 3.03 us
  loops' own time: 4.86 us -> 0 us
    select_n x192 -> x2, other arithmetic: 183 us -> 0.02 us  [the longest x1 0.01 us: local(): wanted = jnp.where(first, places < x, places > x)[:, None, None, None]]
    all_gather x2 -> x0, waiting for transfers between devices: 153 us -> none  [prefix(): everything = lax.all_gather(array, axis)]
    all_gather x0 -> x3, blocking collectives: none -> 44.2 us  [the longest x1 26.6 us: local(): along_z = lax.all_gather(pair.astype(jnp.bfloat16), 'z').astype(jnp.float32)]
    all_to_all x1 -> x0, blocking collectives: 15.4 us -> none  [local(): lax.all_to_all(grad_out, 'head', split_axis=1, concat_axis=0, tiled=True)]
    all_to_all x0 -> x2, waiting for transfers between devices: none -> 11.8 us  [the longest x1 6.71 us: local(): lax.all_to_all(grad_out, 'head', split_axis=1, concat_axis=0, tiled=True)]
    all_to_all x0 -> x2, starting transfers between devices: none -> 11.7 us  [the longest x1 7.65 us: local(): lax.all_to_all(grad_out, 'head', split_axis=1, concat_axis=0, tiled=True)]
    another operation x2 -> x0, loops' own time: 4.86 us -> none  [prefix(): return lax.fori_loop(0, devices, step, start)]
  transfers between devices with their start and end apart: 2 -> 2, of which waited for: 2 -> 2; matrix products, arithmetic and copies ran while one was open for 25% -> 2% of each run, Pallas kernels for 0% -> 0%
where the time goes in v1:
time: 77 us; the launch traced here: 76.7 us
  blocking collectives  44.2 us (57%)
  waiting for transfers between devices  11.8 us (15%)
  starting transfers between devices  11.7 us (15%)
  local copies, waits for them, and re-layouts  4.67 us (6%)
  matrix products  3.03 us (4%)
  between operations  0.8 us (1%)
    all_gather x1, blocking collectives, local(): along_z = lax.all_gather(pair.astype(jnp.bfloat16), 'z').astype(jnp.float32)  26.6 us
    all_gather x2, blocking collectives, from_other_core(): both = lax.all_gather(array, 'c')  17.6 us
    all_to_all x1, starting transfers between devices, local(): lax.all_to_all(grad_out, 'head', split_axis=1, concat_axis=0, tiled=True)  7.65 us
    all_to_all x1, waiting for transfers between devices, local(): lax.all_to_all(grad_out, 'head', split_axis=1, concat_axis=0, tiled=True)  6.71 us
    all_to_all x1, waiting for transfers between devices, local(): lax.all_to_all(jnp.broadcast_to(plane[None], (X, *plane.shape)), 'x', 0,...  5.07 us
    all_to_all x1, starting transfers between devices, local(): lax.all_to_all(jnp.broadcast_to(plane[None], (X, *plane.shape)), 'x', 0,...  4.01 us
    unnamed x9, local copies, waits for them, and re-layouts  2.3 us
    all_to_all x1, local copies, waits for them, and re-layouts, local(): lax.all_to_all(grad_out, 'head', split_axis=1, concat_axis=0, tiled=True)  1.61 us
  transfers between devices with their start and end apart: 2, of which 2 were waited for; matrix products, arithmetic and copies ran while one was open for 2% of the time, Pallas kernels for 0%

profile of v1, /device:TPU:1, one launch (start us, length us, event | category | flops | bytes accessed | tf_op | source)
XLA Modules:
  0.0 76.7 jit_solution(11827741709183489369)
XLA Ops:
  0.6 0.0 copy-start
  0.6 0.0 copy-start.2
  0.7 1.6 %copy.140 = bf16[4,8,8,256]{3,2,0,1:T(8,128)(2,1)} copy(bf16[4,8,8,256]{3,2,1,0:T(8,128)(2,1)} %bitcast.142) | data formatting | bytes 262144 | tf_op jit(solution)/shard_map/all_to_all | solution.py:15
  2.3 7.7 %all-to-all-start = ((bf16[32,8,256]{2,0,1:T(8,128)(2,1)}), bf16[32,8,256]{2,0,1:T(8,128)(2,1)S(1)}, u32[]{:S(2)}, u32[]{:S(2)}) async-start(bf16[32,8,256]{2,0,1:T(8,128)(2,1)} %bitcast.136), calls=%async_computation | async-start | bytes 262144 | tf_op jit(solution)/shard_map/all_to_all | solution.py:15
  10.0 0.0 copy-done
  10.0 1.1 %fusion.16 = f32[2,128,128]{2,1,0:T(8,128)S(1)} fusion(bf16[256,256]{1,0:T(8,128)(2,1)} %param.5, bf16[256,256]{1,0:T(8,128)(2,1)S(1)} %copy-done), kind=kOutput, calls=%fused_computation.28 | convolution fusion | flops 16777216 | bytes 393216 | tf_op jit(solution)/shard_map/htd,hte->hde/dot_general | solution.py:27
  11.1 6.7 %all-to-all-done = bf16[32,8,256]{2,0,1:T(8,128)(2,1)S(1)} async-done(((bf16[32,8,256]{2,0,1:T(8,128)(2,1)}), bf16[32,8,256]{2,0,1:T(8,128)(2,1)S(1)}, u32[]{:S(2)}, u32[]{:S(2)}) %all-to-all-start) | async-done | bytes 131104 | tf_op jit(solution)/shard_map/all_to_all | solution.py:15
  17.9 0.0 copy-done.2
  17.9 0.2 select_convert_fusion
  18.1 8.9 %all-gather = bf16[4,128,128]{2,1,0:T(8,128)(2,1)S(1)} all-gather(bf16[2,128,128]{2,1,0:T(8,128)(2,1)S(1)} %get-tuple-element.17), channel_id=2, replica_groups=mesh['x'=4,'z'=12,'c'=2,'head'=8] {'c'}, dimensions={0}, use_global_device_ids=true | all-gather | bytes 196608 | tf_op jit(solution)/shard_map/all_gather | solution.py:34
  27.0 26.6 %all-gather.1 = bf16[24,128,128]{2,1,0:T(8,128)(2,1)S(1)} all-gather(bf16[2,128,128]{2,1,0:T(8,128)(2,1)S(1)} %fusion.21), channel_id=3, replica_groups=mesh['x'=4,'z'=12,'c'=2,'head'=8] {'z'}, dimensions={0}, use_global_device_ids=true | all-gather | bytes 851968 | tf_op jit(solution)/shard_map/all_gather | solution.py:38
  53.6 0.1 reduce_sum.31
  53.7 0.7 broadcast_in_dim.56
  54.4 4.0 %all-to-all-start.1 = ((bf16[4,2,128,128]{3,2,1,0:T(8,128)(2,1)}), bf16[4,2,128,128]{3,2,1,0:T(8,128)(2,1)S(1)}, u32[]{:S(2)}, u32[]{:S(2)}) async-start(bf16[4,2,128,128]{3,2,1,0:T(8,128)(2,1)} %broadcast_in_dim.56), calls=%async_computation.1 | async-start | bytes 524288 | tf_op jit(solution)/shard_map/all_to_all | solution.py:43
  58.4 0.2 fusion
  58.7 0.2 select_reduce_fusion
  58.9 5.1 %all-to-all-done.1 = bf16[4,2,128,128]{3,2,1,0:T(8,128)(2,1)S(1)} async-done(((bf16[4,2,128,128]{3,2,1,0:T(8,128)(2,1)}), bf16[4,2,128,128]{3,2,1,0:T(8,128)(2,1)S(1)}, u32[]{:S(2)}, u32[]{:S(2)}) %all-to-all-start.1) | async-done | bytes 262176 | tf_op jit(solution)/shard_map/all_to_all | solution.py:43
  64.0 0.1 select_reduce_fusion.1
  64.1 0.0 copy-start.1
  64.1 8.8 %all-gather.2 = bf16[4,128,128]{2,1,0:T(8,128)(2,1)S(1)} all-gather(bf16[2,128,128]{2,1,0:T(8,128)(2,1)S(1)} %get-tuple-element.15), channel_id=4, replica_groups=mesh['x'=4,'z'=12,'c'=2,'head'=8] {'c'}, dimensions={0}, use_global_device_ids=true | all-gather | bytes 196608 | tf_op jit(solution)/shard_map/all_gather | solution.py:34
  72.9 0.2 convolution_bitcast_fusion.4
  73.1 0.2 convolution_bitcast_fusion.3
  73.3 0.0 copy-done.1
  73.3 0.2 convolution_bitcast_fusion.2
  73.5 0.2 fusion.10
  73.8 0.8 copy.54
  74.5 0.2 fusion.11
  74.8 0.8 copy.55
  75.5 0.4 fusion.12
  75.9 0.8 copy.56
  (6 shorter events, 0.1 us)
Async XLA Ops:
  0.6 9.4 %copy-start = (bf16[256,256]{1,0:T(8,128)(2,1)S(1)}, bf16[256,256]{1,0:T(8,128)(2,1)}, u32[]{:S(2)}) copy-start(bf16[256,256]{1,0:T(8,128)(2,1)} %param.6) | copy-start | bytes 393220
  0.6 17.2 %copy-start.2 = (bf16[256,256]{1,0:T(8,128)(2,1)S(1)}, bf16[256,256]{1,0:T(8,128)(2,1)}, u32[]{:S(2)}) copy-start(bf16[256,256]{1,0:T(8,128)(2,1)} %param.4) | copy-start | bytes 393220
  2.3 15.6 %all-to-all-start = ((bf16[32,8,256]{2,0,1:T(8,128)(2,1)}), bf16[32,8,256]{2,0,1:T(8,128)(2,1)S(1)}, u32[]{:S(2)}, u32[]{:S(2)}) async-start(bf16[32,8,256]{2,0,1:T(8,128)(2,1)} %bitcast.136), calls=%async_computation | async-start | bytes 262144 | tf_op jit(solution)/shard_map/all_to_all | solution.py:15
  54.4 9.5 %all-to-all-start.1 = ((bf16[4,2,128,128]{3,2,1,0:T(8,128)(2,1)}), bf16[4,2,128,128]{3,2,1,0:T(8,128)(2,1)S(1)}, u32[]{:S(2)}, u32[]{:S(2)}) async-start(bf16[4,2,128,128]{3,2,1,0:T(8,128)(2,1)} %broadcast_in_dim.56), calls=%async_computation.1 | async-start | bytes 524288 | tf_op jit(solution)/shard_map/all_to_all | solution.py:43
  64.1 9.2 %copy-start.1 = (bf16[256,256]{1,0:T(8,128)(2,1)S(1)}, bf16[256,256]{1,0:T(8,128)(2,1)}, u32[]{:S(2)}) copy-start(bf16[256,256]{1,0:T(8,128)(2,1)} %param.5) | copy-start | bytes 393220

commit v2 on v1

v2 whole, which is shorter than its diff:
```python
import functools
import math

import jax
import jax.numpy as jnp
from jax import lax
from jax.experimental import pallas as pl
from jax.experimental.pallas import tpu as pltpu
from jax.sharding import Mesh
from jax.sharding import PartitionSpec as P

DH = 128
X, ZH, ZL, C = 4, 3, 4, 2
FAR = X * ZH
f32, bf16 = jnp.float32, jnp.bfloat16
VMEM = pl.BlockSpec(memory_space=pltpu.VMEM)
SMEM = pl.BlockSpec(memory_space=pltpu.SMEM)


def call(kernel, name, outs, *args, scalars=0, flops=1_000_000):
    moved = sum(a.size * a.dtype.itemsize for a in args[scalars:])
    moved += sum(math.prod(shape) * jnp.dtype(dtype).itemsize for shape, dtype in outs)
    out = pl.pallas_call(
        kernel,
        out_shape=[jax.ShapeDtypeStruct(shape, dtype) for shape, dtype in outs],
        in_specs=[SMEM] * scalars + [VMEM] * (len(args) - scalars),
        out_specs=[VMEM] * len(outs),
        cost_estimate=pl.CostEstimate(flops=flops, bytes_accessed=moved, transcendentals=0),
        name=name,
    )(*args)
    return out[0] if len(outs) == 1 else out


def dot(a, b, over_a, over_b):
    return lax.dot_general(a, b, (((over_a,), (over_b,)), ((), ())), preferred_element_type=f32)


def head(h):
    return slice(h * DH, (h + 1) * DH)


def spread_kernel(grad_ref, out_ref):
    parts, _, width = out_ref.shape
    for j in range(parts):
        out_ref[j] = grad_ref[:, j * width : (j + 1) * width]


def states_kernel(query_ref, key_ref, value_ref, grad_ref, out_ref):
    for h in range(2):
        out_ref[0, h] = dot(key_ref[:, head(h)], value_ref[:, head(h)], 0, 0)
        out_ref[1, h] = dot(query_ref[:, head(h)], grad_ref[:, head(h)], 0, 0)


def pair_kernel(place_ref, both_ref, out_ref):
    c = place_ref[0]
    for kind in range(2):
        pair = (both_ref[0, kind, c] + both_ref[1, kind, c]).astype(bf16)
        for j in range(ZL):
            out_ref[j, kind] = pair


def blocks_kernel(place_ref, near_ref, out_ref):
    far = place_ref[2]
    block = [sum(near_ref[j, kind].astype(f32) for j in range(ZL)).astype(bf16) for kind in range(2)]
    for p in range(FAR):
        later = far < p

        @pl.when(later)
        def _():
            out_ref[p] = block[0]

        @pl.when(jnp.logical_not(later))
        def _():
            out_ref[p] = block[1]


def inside_kernel(place_ref, both_ref, near_ref, out_ref):
    c, near = place_ref[0], place_ref[1]
    zero = jnp.zeros((DH, DH), f32)
    before = sum(jnp.where(j < near, near_ref[j, 0].astype(f32), zero) for j in range(ZL))
    after = sum(jnp.where(j > near, near_ref[j, 1].astype(f32), zero) for j in range(ZL))
    out_ref[0, 0] = before
    out_ref[1, 0] = before + both_ref[0, 0, c]
    out_ref[0, 1] = after + both_ref[1, 1, c]
    out_ref[1, 1] = after


def local_kernel(query_ref, key_ref, value_ref, grad_ref, dquery_ref, dkey_ref, dvalue_ref):
    tokens = query_ref.shape[0]
    rowidx = lax.broadcasted_iota(jnp.int32, (tokens, tokens), 0)
    colidx = lax.broadcasted_iota(jnp.int32, (tokens, tokens), 1)
    causal = rowidx >= colidx
    for h in range(2):
        q, k, v, g = (r[:, head(h)] for r in (query_ref, key_ref, value_ref, grad_ref))
        score_go = jnp.where(causal, dot(g, v, 1, 1), 0.0).astype(bf16)
        score_qk = jnp.where(causal, dot(q, k, 1, 1), 0.0).astype(bf16)
        dquery_ref[:, head(h)] = dot(score_go, k, 1, 0)
        dkey_ref[:, head(h)] = dot(score_go, q, 0, 0)
        dvalue_ref[:, head(h)] = dot(score_qk, g, 0, 0)


def prefix_kernel(place_ref, far_ref, inside_ref, out_ref):
    far = place_ref[2]
    zero = jnp.zeros((DH, DH), f32)
    before, after = zero, zero
    for p in range(FAR):
        block = far_ref[p].astype(f32)
        before = before + jnp.where(p < far, block, zero)
        after = after + jnp.where(p > far, block, zero)
    for c in range(2):
        out_ref[c, 0] = (inside_ref[c, 0] + before).astype(bf16)
        out_ref[c, 1] = (inside_ref[c, 1] + after).astype(bf16)


def end_kernel(scale, place_ref, key_ref, value_ref, grad_ref, states_ref, *refs):
    local_refs, out_refs = refs[:3], refs[3:]
    c = place_ref[0]
    for h in range(2):
        before, after = states_ref[h, c, 0], states_ref[h, c, 1]
        k, v, g = (r[:, head(h)] for r in (key_ref, value_ref, grad_ref))
        far = (dot(g, before, 1, 1), dot(v, after, 1, 1), dot(k, after, 1, 0))
        for total, local, out in zip(far, local_refs, out_refs):
            out[:, head(h)] = ((total + local[:, head(h)]) * scale).astype(bf16)


def local(query, key, value, grad_out):
    tokens, width = query.shape
    heads = grad_out.shape[1] // width
    x, zh, zl, c = (lax.axis_index(axis) for axis in ("x", "zh", "zl", "c"))
    place = jnp.stack([c, zl, x * ZH + zh]).astype(jnp.int32)
    scale = 1.0 / math.sqrt(DH * tokens * X * ZH * ZL * C)

    spread = call(spread_kernel, "spread", [((heads, tokens // heads, width), bf16)], grad_out)
    grad = lax.all_to_all(spread, "head", 0, 0, tiled=True).reshape(tokens, width)
    states = call(states_kernel, "states", [((2, 2, DH, DH), f32)], query, key, value, grad)
    both = lax.all_gather(states, "c")
    pair = call(pair_kernel, "pair", [((ZL, 2, DH, DH), bf16)], place, both, scalars=1)
    near = lax.all_to_all(pair, "zl", 0, 0, tiled=True)
    block = call(blocks_kernel, "blocks", [((FAR, DH, DH), bf16)], place, near, scalars=1)
    far = lax.all_to_all(block, ("x", "zh"), 0, 0, tiled=True)
    inside = call(
        inside_kernel, "inside", [((2, 2, DH, DH), f32)], place, both, near, scalars=1
    )
    partial = call(
        local_kernel, "local", [((tokens, width), f32)] * 3, query, key, value, grad, flops=200_000_000
    )
    mine = call(prefix_kernel, "prefix", [((2, 2, DH, DH), bf16)], place, far, inside, scalars=1)
    ends = lax.all_gather(mine, "c")
    outs = call(
        functools.partial(end_kernel, scale),
        "end",
        [((tokens, width), bf16)] * 3,
        place,
        key,
        value,
        grad,
        ends,
        *partial,
        scalars=1,
    )
    return tuple(outs)


def solution(mesh):
    split = Mesh(mesh.devices.reshape(X, ZH, ZL, C, -1), ("x", "zh", "zl", "c", "head"))
    rows = ("x", "zh", "zl", "c")
    placed = (P(rows, "head"),) * 3
    return jax.shard_map(
        local,
        mesh=split,
        in_specs=(*placed, P((*rows, "head"), None)),
        out_specs=placed,
        check_vma=False,
    )
```

time: 77 us -> 88.5 us (1.15)
  Pallas kernels: 0 us -> 16.1 us
  blocking collectives: 44.2 us -> 29.7 us
  waiting for transfers between devices: 11.8 us -> 21.3 us
  starting transfers between devices: 11.7 us -> 17.9 us
  local copies, waits for them, and re-layouts: 4.67 us -> 1.4 us
  matrix products: 3.03 us -> 0 us
    all_gather x3 -> x2, blocking collectives: 44.2 us -> 17.4 us  [the longest x1 12.3 us: local(): both = lax.all_gather(states, 'c')]
    pallas_call x0 -> x8, Pallas kernels: none -> 16.1 us  [call(): pl.pallas_call(kernel, out_shape=[jax.ShapeDtypeStruct(shape, dtype) for...]
    all_to_all x0 -> x1, blocking collectives: none -> 12.3 us  [local(): near = lax.all_to_all(pair, 'zl', 0, 0, tiled=True)]
    all_to_all x2, waiting for transfers between devices: 11.8 us -> 21.3 us  [the longest x1 14 us: local(): far = lax.all_to_all(block, ('x', 'zh'), 0, 0, tiled=True)]
    all_to_all x2, starting transfers between devices: 11.7 us -> 17.9 us  [the longest x1 10.3 us: local(): far = lax.all_to_all(block, ('x', 'zh'), 0, 0, tiled=True)]
    dot_general x9 -> x0, matrix products: 3.03 us -> none  [the longest x1 1.13 us: local(): jnp.einsum('htd,hte->hde', key_rows, value_rows, preferred_element_type=j...]
    all_to_all x1 -> x0, local copies, waits for them, and re-layouts: 1.61 us -> none  [local(): lax.all_to_all(grad_out, 'head', split_axis=1, concat_axis=0, tiled=True)]
    unnamed x9 -> x4, local copies, waits for them, and re-layouts: 2.3 us -> 1.4 us
  transfers between devices with their start and end apart: 2 -> 2, of which waited for: 2 -> 2; matrix products, arithmetic and copies ran while one was open for 2% -> 1% of each run, Pallas kernels for 0% -> 5%
where the time goes in v2:
time: 88.5 us; the launch traced here: 87.7 us
  blocking collectives  29.7 us (34%)
  waiting for transfers between devices  21.3 us (24%)
  starting transfers between devices  17.9 us (20%)
  Pallas kernels  16.1 us (18%)
  local copies, waits for them, and re-layouts  1.4 us (2%)
    pallas_call x8, Pallas kernels, call(): pl.pallas_call(kernel, out_shape=[jax.ShapeDtypeStruct(shape, dtype) for...  16.1 us
    all_to_all x1, waiting for transfers between devices, local(): far = lax.all_to_all(block, ('x', 'zh'), 0, 0, tiled=True)  14 us
    all_to_all x1, blocking collectives, local(): near = lax.all_to_all(pair, 'zl', 0, 0, tiled=True)  12.3 us
    all_gather x1, blocking collectives, local(): both = lax.all_gather(states, 'c')  12.3 us
    all_to_all x1, starting transfers between devices, local(): far = lax.all_to_all(block, ('x', 'zh'), 0, 0, tiled=True)  10.3 us
    all_to_all x1, starting transfers between devices, local(): lax.all_to_all(spread, 'head', 0, 0, tiled=True).reshape(tokens, width)  7.65 us
    all_to_all x1, waiting for transfers between devices, local(): lax.all_to_all(spread, 'head', 0, 0, tiled=True).reshape(tokens, width)  7.33 us
    all_gather x1, blocking collectives, local(): ends = lax.all_gather(mine, 'c')  5.1 us
  transfers between devices with their start and end apart: 2, of which 2 were waited for; matrix products, arithmetic and copies ran while one was open for 1% of the time, Pallas kernels for 5%

profile of v2, /device:TPU:1, one launch (start us, length us, event | category | flops | bytes accessed | tf_op | source)
XLA Modules:
  0.0 87.7 jit_solution(2153203922860871383)
XLA Ops:
  0.6 1.6 %spread.1 = bf16[8,32,256]{2,1,0:T(8,128)(2,1)} custom-call(bf16[32,2048]{1,0:T(8,128)(2,1)} %grad_ref.1), custom_call_target="tpu_custom_call" | custom-call | flops 1000000 | bytes 262144 | tf_op jit(solution)/shard_map/spread/pallas_call | solution.py:23
  2.2 7.7 %all-to-all-start = ((bf16[8,32,256]{2,1,0:T(8,128)(2,1)}), bf16[8,32,256]{2,1,0:T(8,128)(2,1)S(1)}, u32[]{:S(2)}, u32[]{:S(2)}) async-start(bf16[8,32,256]{2,1,0:T(8,128)(2,1)} %spread.1), calls=%async_computation | async-start | bytes 262144 | tf_op jit(solution)/shard_map/all_to_all | solution.py:134
  9.8 0.6 pad_add_fusion.place_ref
  10.4 7.3 %all-to-all-done = bf16[8,32,256]{2,1,0:T(8,128)(2,1)S(1)} async-done(((bf16[8,32,256]{2,1,0:T(8,128)(2,1)}), bf16[8,32,256]{2,1,0:T(8,128)(2,1)S(1)}, u32[]{:S(2)}, u32[]{:S(2)}) %all-to-all-start) | async-done | bytes 131104 | tf_op jit(solution)/shard_map/all_to_all | solution.py:134
  17.8 0.0 copy-start.1
  17.8 0.6 copy-done.1
  18.4 2.1 %states.1 = f32[2,2,128,128]{3,2,1,0:T(8,128)} custom-call(bf16[256,256]{1,0:T(8,128)(2,1)} %query_ref.3, bf16[256,256]{1,0:T(8,128)(2,1)} %key_ref.5, bf16[256,256]{1,0:T(8,128)(2,1)} %value_ref.5, bf16[256,256]{1,0:T(8,128)(2,1)} %bitcast.8), custom_call_target="tpu_custom_call" | custom-call | flops 1000000 | bytes 786432 | tf_op jit(solution)/shard_map/states/pallas_call | solution.py:23
  20.5 12.3 %all-gather = f32[4,2,128,128]{3,2,1,0:T(8,128)} all-gather(f32[2,2,128,128]{3,2,1,0:T(8,128)} %states.1), channel_id=2, replica_groups=mesh['x'=4,'zh'=3,'zl'=4,'c'=2,'head'=8] {'c'}, dimensions={0}, use_global_device_ids=true | all-gather | bytes 786432 | tf_op jit(solution)/shard_map/all_gather | solution.py:136
  32.8 1.8 %pair.1 = bf16[4,2,128,128]{3,2,1,0:T(8,128)(2,1)} custom-call(s32[3]{0:T(128)} %pad_add_fusion.place_ref, f32[2,2,2,128,128]{4,3,2,1,0:T(8,128)} %bitcast.6), custom_call_target="tpu_custom_call" | custom-call | flops 1000000 | bytes 786432 | tf_op jit(solution)/shard_map/pair/pallas_call | solution.py:23
  34.5 12.3 %all_to_all.15.near_ref = bf16[4,2,128,128]{3,2,1,0:T(8,128)(2,1)} all-to-all(bf16[4,2,128,128]{3,2,1,0:T(8,128)(2,1)} %pair.1), channel_id=1, replica_groups=mesh['x'=4,'zh'=3,'zl'=4,'c'=2,'head'=8] {'zl'}, dimensions={0} | all-to-all | bytes 524288 | tf_op jit(solution)/shard_map/all_to_all | solution.py:138
  46.9 1.9 %blocks.1 = bf16[12,128,128]{2,1,0:T(8,128)(2,1)} custom-call(s32[3]{0:T(128)} %pad_add_fusion.place_ref, bf16[4,2,128,128]{3,2,1,0:T(8,128)(2,1)} %all_to_all.15.near_ref), custom_call_target="tpu_custom_call" | custom-call | flops 1000000 | bytes 655360 | tf_op jit(solution)/shard_map/blocks/pallas_call | solution.py:23
  48.7 10.3 %all-to-all-start.2 = ((bf16[12,128,128]{2,1,0:T(8,128)(2,1)}), bf16[12,128,128]{2,1,0:T(8,128)(2,1)S(1)}, u32[]{:S(2)}, u32[]{:S(2)}) async-start(bf16[12,128,128]{2,1,0:T(8,128)(2,1)} %blocks.1), calls=%async_computation.2 | async-start | bytes 786432 | tf_op jit(solution)/shard_map/all_to_all | solution.py:140
  59.0 2.7 %local.1 = (f32[256,256]{1,0:T(8,128)}, f32[256,256]{1,0:T(8,128)}, f32[256,256]{1,0:T(8,128)}) custom-call(bf16[256,256]{1,0:T(8,128)(2,1)} %query_ref.3, bf16[256,256]{1,0:T(8,128)(2,1)} %key_ref.5, bf16[256,256]{1,0:T(8,128)(2,1)} %value_ref.5, bf16[256,256]{1,0:T(8,128)(2,1)} %bitcast.9), custom_call_target="tpu_custom_call" | custom-call | flops 200000000 | bytes 1310720 | tf_op jit(solution)/shard_map/local/pallas_call | solution.py:23
  61.8 1.9 %inside.1.inside_ref = f32[2,2,128,128]{3,2,1,0:T(8,128)} custom-call(s32[3]{0:T(128)} %pad_add_fusion.place_ref, f32[2,2,2,128,128]{4,3,2,1,0:T(8,128)} %bitcast.7, bf16[4,2,128,128]{3,2,1,0:T(8,128)(2,1)} %all_to_all.15.near_ref), custom_call_target="tpu_custom_call" | custom-call | flops 1000000 | bytes 1048576 | tf_op jit(solution)/shard_map/inside/pallas_call | solution.py:23
  63.6 14.0 %all-to-all-done.2.far_ref = bf16[12,128,128]{2,1,0:T(8,128)(2,1)S(1)} async-done(((bf16[12,128,128]{2,1,0:T(8,128)(2,1)}), bf16[12,128,128]{2,1,0:T(8,128)(2,1)S(1)}, u32[]{:S(2)}, u32[]{:S(2)}) %all-to-all-start.2) | async-done | bytes 393248 | tf_op jit(solution)/shard_map/all_to_all | solution.py:140
  77.7 0.0 copy-start
  77.7 0.8 copy-done
  78.4 1.9 %prefix.1 = bf16[2,2,128,128]{3,2,1,0:T(8,128)(2,1)} custom-call(s32[3]{0:T(128)} %pad_add_fusion.place_ref, bf16[12,128,128]{2,1,0:T(8,128)(2,1)} %copy-done, f32[2,2,128,128]{3,2,1,0:T(8,128)} %inside.1.inside_ref), custom_call_target="tpu_custom_call" | custom-call | flops 1000000 | bytes 786432 | tf_op jit(solution)/shard_map/prefix/pallas_call | solution.py:23
  80.3 5.1 %all-gather.1 = bf16[4,2,128,128]{3,2,1,0:T(8,128)(2,1)} all-gather(bf16[2,2,128,128]{3,2,1,0:T(8,128)(2,1)} %prefix.1), channel_id=3, replica_groups=mesh['x'=4,'zh'=3,'zl'=4,'c'=2,'head'=8] {'c'}, dimensions={0}, use_global_device_ids=true | all-gather | bytes 393216 | tf_op jit(solution)/shard_map/all_gather | solution.py:148
  85.4 2.3 %end.1 = (bf16[256,256]{1,0:T(8,128)(2,1)}, bf16[256,256]{1,0:T(8,128)(2,1)}, bf16[256,256]{1,0:T(8,128)(2,1)}) custom-call(s32[3]{0:T(128)} %pad_add_fusion.place_ref, bf16[256,256]{1,0:T(8,128)(2,1)} %key_ref.5, bf16[256,256]{1,0:T(8,128)(2,1)} %value_ref.5, bf16[256,256]{1,0:T(8,128)(2,1)} %bitcast.10, bf16[2,2,2,128,128]{4,3,2,1,0:T(8,128)(2,1)} %bitcast.11, ...), custom_call_target="tpu_custom_call" | custom-call | flops 1000000 | bytes 1835008 | tf_op jit(solution)/shard_map/end/pallas_call | solution.py:23
Async XLA Ops:
  2.2 15.6 %all-to-all-start = ((bf16[8,32,256]{2,1,0:T(8,128)(2,1)}), bf16[8,32,256]{2,1,0:T(8,128)(2,1)S(1)}, u32[]{:S(2)}, u32[]{:S(2)}) async-start(bf16[8,32,256]{2,1,0:T(8,128)(2,1)} %spread.1), calls=%async_computation | async-start | bytes 262144 | tf_op jit(solution)/shard_map/all_to_all | solution.py:134
  17.8 0.6 copy-start.1
  48.7 28.9 %all-to-all-start.2 = ((bf16[12,128,128]{2,1,0:T(8,128)(2,1)}), bf16[12,128,128]{2,1,0:T(8,128)(2,1)S(1)}, u32[]{:S(2)}, u32[]{:S(2)}) async-start(bf16[12,128,128]{2,1,0:T(8,128)(2,1)} %blocks.1), calls=%async_computation.2 | async-start | bytes 786432 | tf_op jit(solution)/shard_map/all_to_all | solution.py:140
  77.7 0.8 copy-start

commit v3 on v2

v3 whole, which is shorter than its diff:
```python
import functools
import math

import jax
import jax.numpy as jnp
from jax import lax
from jax.experimental import pallas as pl
from jax.experimental.pallas import tpu as pltpu
from jax.sharding import Mesh
from jax.sharding import PartitionSpec as P

DH = 128
X, ZH, ZL, C = 4, 3, 4, 2
NEAR, FAR = ZL * C, X * ZH
ROOM = 8 << 20
f32, bf16 = jnp.float32, jnp.bfloat16
VMEM = pl.BlockSpec(memory_space=pltpu.VMEM)
ANY = pl.BlockSpec(memory_space=pl.ANY)


def call(kernel, name, outs, *args, space=VMEM, flops=1_000_000, scratch=()):
    moved = sum(a.size * a.dtype.itemsize for a in args)
    moved += sum(math.prod(shape) * jnp.dtype(dtype).itemsize for shape, dtype in outs)
    out = pl.pallas_call(
        kernel,
        out_shape=[jax.ShapeDtypeStruct(shape, dtype) for shape, dtype in outs],
        in_specs=[space] * len(args),
        out_specs=[space] * len(outs),
        scratch_shapes=scratch,
        compiler_params=pltpu.CompilerParams(vmem_limit_bytes=ROOM),
        cost_estimate=pl.CostEstimate(flops=flops, bytes_accessed=moved, transcendentals=0),
        name=name,
    )(*args)
    return out[0] if len(outs) == 1 else out


def dot(a, b, over_a, over_b):
    return lax.dot_general(a, b, (((over_a,), (over_b,)), ((), ())), preferred_element_type=f32)


def head(h):
    return slice(h * DH, (h + 1) * DH)


def block_index():
    return lax.axis_index("x") * ZH + lax.axis_index("zh")


def spread_kernel(grad_ref, out_ref, sems):
    parts, _, width = out_ref.shape
    copies = [
        pltpu.make_async_copy(
            grad_ref.at[:, j * width : (j + 1) * width], out_ref.at[j], sems.at[j]
        )
        for j in range(parts)
    ]
    for copy in copies:
        copy.start()
    for copy in copies:
        copy.wait()


def states_kernel(query_ref, key_ref, value_ref, grad_ref, out_ref):
    per_head, rows = NEAR // 2, 2 * DH // NEAR
    for h in range(2):
        kv = dot(key_ref[:, head(h)], value_ref[:, head(h)], 0, 0)
        qg = dot(query_ref[:, head(h)], grad_ref[:, head(h)], 0, 0)
        for kind, state in enumerate((kv, qg)):
            out_ref[h * per_head : (h + 1) * per_head, kind] = state.astype(
                out_ref.dtype
            ).reshape(per_head, rows, DH)


def blocks_kernel(near_ref, out_ref):
    me = block_index()
    kv, qg = (
        sum(near_ref[i, kind].astype(f32) for i in range(NEAR)).astype(out_ref.dtype)
        for kind in range(2)
    )
    for p in range(FAR):
        out_ref[p] = jnp.where(me < p, kv, qg)


def inside_kernel(near_ref, out_ref):
    zero = jnp.zeros(near_ref.shape[2:], f32)
    before, after = zero, zero
    for i in range(NEAR):
        last = NEAR - 1 - i
        out_ref[i, 0] = before
        out_ref[last, 1] = after
        before = before + near_ref[i, 0].astype(f32)
        after = after + near_ref[last, 1].astype(f32)


def local_kernel(query_ref, key_ref, value_ref, grad_ref, dquery_ref, dkey_ref, dvalue_ref):
    tokens = query_ref.shape[0]
    rowidx = lax.broadcasted_iota(jnp.int32, (tokens, tokens), 0)
    colidx = lax.broadcasted_iota(jnp.int32, (tokens, tokens), 1)
    causal = rowidx >= colidx
    for h in range(2):
        q, k, v, g = (r[:, head(h)] for r in (query_ref, key_ref, value_ref, grad_ref))
        score_go = jnp.where(causal, dot(g, v, 1, 1), 0.0).astype(bf16)
        score_qk = jnp.where(causal, dot(q, k, 1, 1), 0.0).astype(bf16)
        dquery_ref[:, head(h)] = dot(score_go, k, 1, 0)
        dkey_ref[:, head(h)] = dot(score_go, q, 0, 0)
        dvalue_ref[:, head(h)] = dot(score_qk, g, 0, 0)


def prefix_kernel(far_ref, inside_ref, out_ref):
    me = block_index()
    zero = jnp.zeros(far_ref.shape[1:], f32)
    before, after = zero, zero
    for p in range(FAR):
        block = far_ref[p].astype(f32)
        before = before + jnp.where(p < me, block, zero)
        after = after + jnp.where(p > me, block, zero)
    for i in range(NEAR):
        out_ref[i, 0] = (inside_ref[i, 0] + before).astype(bf16)
        out_ref[i, 1] = (inside_ref[i, 1] + after).astype(bf16)


def end_kernel(scale, key_ref, value_ref, grad_ref, states_ref, *refs):
    local_refs, out_refs = refs[:3], refs[3:]
    per_head = NEAR // 2
    for h in range(2):
        before, after = (
            states_ref[h * per_head : (h + 1) * per_head, kind].reshape(DH, DH)
            for kind in range(2)
        )
        k, v, g = (r[:, head(h)] for r in (key_ref, value_ref, grad_ref))
        far = (dot(g, before, 1, 1), dot(v, after, 1, 1), dot(k, after, 1, 0))
        for total, local, out in zip(far, local_refs, out_refs):
            out[:, head(h)] = ((total + local[:, head(h)]) * scale).astype(bf16)


def local(query, key, value, grad_out):
    tokens, width = query.shape
    heads = grad_out.shape[1] // width
    rows = 2 * DH // NEAR
    scale = 1.0 / math.sqrt(DH * tokens * X * ZH * ZL * C)

    spread = call(
        spread_kernel,
        "spread",
        [((heads, tokens // heads, width), bf16)],
        grad_out,
        space=ANY,
        scratch=[pltpu.SemaphoreType.DMA((heads,))],
    )
    grad = lax.all_to_all(spread, "head", 0, 0, tiled=True).reshape(tokens, width)
    states = call(
        states_kernel, "states", [((NEAR, 2, rows, DH), bf16)], query, key, value, grad
    )
    near = lax.all_to_all(states, ("zl", "c"), 0, 0, tiled=True)
    block = call(blocks_kernel, "blocks", [((FAR, rows, DH), bf16)], near)
    far = lax.all_to_all(block, ("x", "zh"), 0, 0, tiled=True)
    inside = call(inside_kernel, "inside", [((NEAR, 2, rows, DH), f32)], near)
    partial = call(
        local_kernel, "local", [((tokens, width), f32)] * 3, query, key, value, grad, flops=200_000_000
    )
    mine = call(prefix_kernel, "prefix", [((NEAR, 2, rows, DH), bf16)], far, inside)
    ends = lax.all_to_all(mine, ("zl", "c"), 0, 0, tiled=True)
    outs = call(
        functools.partial(end_kernel, scale),
        "end",
        [((tokens, width), bf16)] * 3,
        key,
        value,
        grad,
        ends,
        *partial,
    )
    return tuple(outs)


def solution(mesh):
    split = Mesh(mesh.devices.reshape(X, ZH, ZL, C, -1), ("x", "zh", "zl", "c", "head"))
    rows = ("x", "zh", "zl", "c")
    placed = (P(rows, "head"),) * 3
    return jax.shard_map(
        local,
        mesh=split,
        in_specs=(*placed, P((*rows, "head"), None)),
        out_specs=placed,
        check_vma=False,
    )
```

time: 88.5 us -> 69.9 us (0.79)
  Pallas kernels: 16.1 us -> 3.59 us
  waiting for transfers between devices: 21.3 us -> 14.4 us
  starting transfers between devices: 17.9 us -> 19.4 us
    all_to_all x1 -> x2, blocking collectives: 12.3 us -> 30.5 us  [the longest x1 15.5 us: local(): lax.all_to_all(spread, 'head', 0, 0, tiled=True).reshape(tokens, width)]
    all_gather x2 -> x0, blocking collectives: 17.4 us -> none  [the longest x1 12.3 us: local(): both = lax.all_gather(states, 'c')]
    pallas_call x8 -> x7, Pallas kernels: 16.1 us -> 3.59 us  [call(): pl.pallas_call(kernel, out_shape=[jax.ShapeDtypeStruct(shape, dtype) for...]
    all_to_all x1, waiting for transfers between devices: 14 us -> 9.39 us  [local(): far = lax.all_to_all(block, ('x', 'zh'), 0, 0, tiled=True)]
    all_to_all x1, starting transfers between devices: 10.3 us -> 13.4 us  [local(): far = lax.all_to_all(block, ('x', 'zh'), 0, 0, tiled=True)]
    all_to_all x1, waiting for transfers between devices: 7.33 us -> 5.02 us  [local(): ends = lax.all_to_all(mine, ('zl', 'c'), 0, 0, tiled=True)]
    all_to_all x1, starting transfers between devices: 7.65 us -> 5.98 us  [local(): ends = lax.all_to_all(mine, ('zl', 'c'), 0, 0, tiled=True)]
  transfers between devices with their start and end apart: 2 -> 2, of which waited for: 2 -> 2; matrix products, arithmetic and copies ran while one was open for 1% -> 0% of each run, Pallas kernels for 5% -> 1%
where the time goes in v3:
time: 69.9 us; the launch traced here: 69.5 us
  blocking collectives  30.5 us (44%)
  starting transfers between devices  19.4 us (28%)
  waiting for transfers between devices  14.4 us (21%)
  Pallas kernels  3.59 us (5%)
  local copies, waits for them, and re-layouts  0.91 us (1%)
  between operations  0.7 us (1%)
    all_to_all x1, blocking collectives, local(): lax.all_to_all(spread, 'head', 0, 0, tiled=True).reshape(tokens, width)  15.5 us
    all_to_all x1, blocking collectives, local(): near = lax.all_to_all(states, ('zl', 'c'), 0, 0, tiled=True)  15 us
    all_to_all x1, starting transfers between devices, local(): far = lax.all_to_all(block, ('x', 'zh'), 0, 0, tiled=True)  13.4 us
    all_to_all x1, waiting for transfers between devices, local(): far = lax.all_to_all(block, ('x', 'zh'), 0, 0, tiled=True)  9.39 us
    all_to_all x1, starting transfers between devices, local(): ends = lax.all_to_all(mine, ('zl', 'c'), 0, 0, tiled=True)  5.98 us
    all_to_all x1, waiting for transfers between devices, local(): ends = lax.all_to_all(mine, ('zl', 'c'), 0, 0, tiled=True)  5.02 us
    pallas_call x7, Pallas kernels, call(): pl.pallas_call(kernel, out_shape=[jax.ShapeDtypeStruct(shape, dtype) for...  3.59 us
  transfers between devices with their start and end apart: 2, of which 2 were waited for; matrix products, arithmetic and copies ran while one was open for 0% of the time, Pallas kernels for 1%

profile of v3, /device:TPU:1, one launch (start us, length us, event | category | flops | bytes accessed | tf_op | source)
XLA Modules:
  0.0 69.5 jit_solution(7287020674940615968)
XLA Ops:
  0.6 0.0 copy-start.3
  0.6 0.9 %copy-done.3 = bf16[32,2048]{1,0:T(8,128)(2,1)S(1)} copy-done((bf16[32,2048]{1,0:T(8,128)(2,1)S(1)}, bf16[32,2048]{1,0:T(8,128)(2,1)}, u32[]{:S(2)}) %copy-start.3) | copy-done | bytes 131096
  1.5 0.0 copy-start.2
  1.5 0.1 spread.1
  1.7 0.0 copy-start
  1.7 0.0 copy-start.1
  1.7 15.5 %all_to_all.20 = bf16[8,32,256]{2,1,0:T(8,128)(2,1)S(1)} all-to-all(bf16[8,32,256]{2,1,0:T(8,128)(2,1)S(1)} %spread.1), channel_id=1, replica_groups=mesh['x'=4,'zh'=3,'zl'=4,'c'=2,'head'=8] {'head'}, dimensions={0} | all-to-all | bytes 262144 | tf_op jit(solution)/shard_map/all_to_all | solution.py:150
  17.2 0.0 copy-done.2
  17.2 0.0 copy-done
  17.2 0.0 copy-done.1
  17.2 0.3 states.1
  17.5 15.0 %all_to_all.21.near_ref = bf16[8,2,32,128]{3,2,1,0:T(8,128)(2,1)S(1)} all-to-all(bf16[8,2,32,128]{3,2,1,0:T(8,128)(2,1)S(1)} %states.1), channel_id=1, replica_groups=mesh['x'=4,'zh'=3,'zl'=4,'c'=2,'head'=8] {'zl','c'}, dimensions={0} | all-to-all | bytes 262144 | tf_op jit(solution)/shard_map/all_to_all | solution.py:154
  32.5 0.7 blocks.1
  33.2 13.4 %all-to-all-start.2 = ((bf16[12,32,128]{2,1,0:T(8,128)(2,1)}), bf16[12,32,128]{2,1,0:T(8,128)(2,1)S(1)}, u32[]{:S(2)}, u32[]{:S(2)}) async-start(bf16[12,32,128]{2,1,0:T(8,128)(2,1)} %blocks.1), calls=%async_computation.2 | async-start | bytes 196608 | tf_op jit(solution)/shard_map/all_to_all | solution.py:156
  46.6 9.4 %all-to-all-done.2.far_ref = bf16[12,32,128]{2,1,0:T(8,128)(2,1)S(1)} async-done(((bf16[12,32,128]{2,1,0:T(8,128)(2,1)}), bf16[12,32,128]{2,1,0:T(8,128)(2,1)S(1)}, u32[]{:S(2)}, u32[]{:S(2)}) %all-to-all-start.2) | async-done | bytes 98336 | tf_op jit(solution)/shard_map/all_to_all | solution.py:156
  56.0 0.7 %prefix.1 = bf16[8,2,32,128]{3,2,1,0:T(8,128)(2,1)} custom-call(bf16[12,32,128]{2,1,0:T(8,128)(2,1)S(1)} %all-to-all-done.2.far_ref, f32[8,2,32,128]{3,2,1,0:T(8,128)S(1)} %inside.1.inside_ref), custom_call_target="tpu_custom_call" | custom-call | flops 1000000 | bytes 491520 | tf_op jit(solution)/shard_map/prefix/pallas_call | solution.py:24
  56.7 6.0 %all-to-all-start.3 = ((bf16[8,2,32,128]{3,2,1,0:T(8,128)(2,1)}), bf16[8,2,32,128]{3,2,1,0:T(8,128)(2,1)S(1)}, u32[]{:S(2)}, u32[]{:S(2)}) async-start(bf16[8,2,32,128]{3,2,1,0:T(8,128)(2,1)} %prefix.1), calls=%async_computation.3 | async-start | bytes 262144 | tf_op jit(solution)/shard_map/all_to_all | solution.py:162
  62.7 0.8 %local.1 = (f32[256,256]{1,0:T(8,128)S(1)}, f32[256,256]{1,0:T(8,128)S(1)}, f32[256,256]{1,0:T(8,128)S(1)}) custom-call(bf16[256,256]{1,0:T(8,128)(2,1)S(1)} %copy-done.2, bf16[256,256]{1,0:T(8,128)(2,1)S(1)} %copy-done, bf16[256,256]{1,0:T(8,128)(2,1)S(1)} %copy-done.1, bf16[256,256]{1,0:T(8,128)(2,1)S(1)} %bitcast.2), custom_call_target="tpu_custom_call" | custom-call | flops 200000000 | bytes 1310720 | tf_op jit(solution)/shard_map/local/pallas_call | solution.py:24
  63.5 5.0 %all-to-all-done.3.states_ref = bf16[8,2,32,128]{3,2,1,0:T(8,128)(2,1)S(1)} async-done(((bf16[8,2,32,128]{3,2,1,0:T(8,128)(2,1)}), bf16[8,2,32,128]{3,2,1,0:T(8,128)(2,1)S(1)}, u32[]{:S(2)}, u32[]{:S(2)}) %all-to-all-start.3) | async-done | bytes 131104 | tf_op jit(solution)/shard_map/all_to_all | solution.py:162
  68.6 1.0 %end.1 = (bf16[256,256]{1,0:T(8,128)(2,1)}, bf16[256,256]{1,0:T(8,128)(2,1)}, bf16[256,256]{1,0:T(8,128)(2,1)}) custom-call(bf16[256,256]{1,0:T(8,128)(2,1)S(1)} %copy-done, bf16[256,256]{1,0:T(8,128)(2,1)S(1)} %copy-done.1, bf16[256,256]{1,0:T(8,128)(2,1)S(1)} %bitcast.3, bf16[8,2,32,128]{3,2,1,0:T(8,128)(2,1)S(1)} %all-to-all-done.3.states_ref, ...), custom_call_target="tpu_custom_call" | custom-call | flops 1000000 | bytes 1703936 | tf_op jit(solution)/shard_map/end/pallas_call | solution.py:24
  (1 shorter events, 0.0 us)
Async XLA Ops:
  0.6 0.9 %copy-start.3 = (bf16[32,2048]{1,0:T(8,128)(2,1)S(1)}, bf16[32,2048]{1,0:T(8,128)(2,1)}, u32[]{:S(2)}) copy-start(bf16[32,2048]{1,0:T(8,128)(2,1)} %grad_ref.1) | copy-start | bytes 393220
  1.5 15.7 %copy-start.2 = (bf16[256,256]{1,0:T(8,128)(2,1)S(1)}, bf16[256,256]{1,0:T(8,128)(2,1)}, u32[]{:S(2)}) copy-start(bf16[256,256]{1,0:T(8,128)(2,1)} %query_ref.3) | copy-start | bytes 393220
  1.7 15.5 %copy-start = (bf16[256,256]{1,0:T(8,128)(2,1)S(1)}, bf16[256,256]{1,0:T(8,128)(2,1)}, u32[]{:S(2)}) copy-start(bf16[256,256]{1,0:T(8,128)(2,1)} %key_ref.5) | copy-start | bytes 393220
  1.7 15.5 %copy-start.1 = (bf16[256,256]{1,0:T(8,128)(2,1)S(1)}, bf16[256,256]{1,0:T(8,128)(2,1)}, u32[]{:S(2)}) copy-start(bf16[256,256]{1,0:T(8,128)(2,1)} %value_ref.5) | copy-start | bytes 393220
  33.2 22.9 %all-to-all-start.2 = ((bf16[12,32,128]{2,1,0:T(8,128)(2,1)}), bf16[12,32,128]{2,1,0:T(8,128)(2,1)S(1)}, u32[]{:S(2)}, u32[]{:S(2)}) async-start(bf16[12,32,128]{2,1,0:T(8,128)(2,1)} %blocks.1), calls=%async_computation.2 | async-start | bytes 196608 | tf_op jit(solution)/shard_map/all_to_all | solution.py:156
  56.7 11.8 %all-to-all-start.3 = ((bf16[8,2,32,128]{3,2,1,0:T(8,128)(2,1)}), bf16[8,2,32,128]{3,2,1,0:T(8,128)(2,1)S(1)}, u32[]{:S(2)}, u32[]{:S(2)}) async-start(bf16[8,2,32,128]{3,2,1,0:T(8,128)(2,1)} %prefix.1), calls=%async_computation.3 | async-start | bytes 262144 | tf_op jit(solution)/shard_map/all_to_all | solution.py:162

commit v4 on v3

--- a/solution.py
+++ b/solution.py
@@ -13,6 +13,14 @@
 X, ZH, ZL, C = 4, 3, 4, 2
 NEAR, FAR = ZL * C, X * ZH
 ROOM = 8 << 20
+NEAR_ORDER = [7, 6, 5, 4, 3, 2, 1, 0]
+FAR_ORDER = [8, 11, 10, 9, 7, 6, 5, 4, 3, 2, 1, 0]
+HEAD_ORDER = [4, 3, 5, 2, 6, 1, 7, 0]
+HEADS = len(HEAD_ORDER)
+HEAD_AT = [HEAD_ORDER.index(i) for i in range(HEADS)]
+NEAR_AT = [NEAR_ORDER.index(i) for i in range(NEAR)]
+NEAR_GROUPS = [[(f * NEAR) + i for i in NEAR_ORDER] for f in range(FAR)]
+FAR_GROUPS = [[f * NEAR + i for f in FAR_ORDER] for i in range(NEAR)]
 f32, bf16 = jnp.float32, jnp.bfloat16
 VMEM = pl.BlockSpec(memory_space=pltpu.VMEM)
 ANY = pl.BlockSpec(memory_space=pl.ANY)
@@ -42,15 +50,19 @@
     return slice(h * DH, (h + 1) * DH)
 
 
+def rows_of(grad_ref):
+    return jnp.concatenate([grad_ref[HEAD_AT[t]] for t in range(HEADS)], axis=0)
+
+
 def block_index():
-    return lax.axis_index("x") * ZH + lax.axis_index("zh")
+    return lax.axis_index("seq") // NEAR
 
 
 def spread_kernel(grad_ref, out_ref, sems):
     parts, _, width = out_ref.shape
     copies = [
         pltpu.make_async_copy(
-            grad_ref.at[:, j * width : (j + 1) * width], out_ref.at[j], sems.at[j]
+            grad_ref.at[:, j * width : (j + 1) * width], out_ref.at[HEAD_AT[j]], sems.at[j]
         )
         for j in range(parts)
     ]
@@ -62,9 +74,10 @@
 
 def states_kernel(query_ref, key_ref, value_ref, grad_ref, out_ref):
     per_head, rows = NEAR // 2, 2 * DH // NEAR
+    grad = rows_of(grad_ref)
     for h in range(2):
         kv = dot(key_ref[:, head(h)], value_ref[:, head(h)], 0, 0)
-        qg = dot(query_ref[:, head(h)], grad_ref[:, head(h)], 0, 0)
+        qg = dot(query_ref[:, head(h)], grad[:, head(h)], 0, 0)
         for kind, state in enumerate((kv, qg)):
             out_ref[h * per_head : (h + 1) * per_head, kind] = state.astype(
                 out_ref.dtype
@@ -78,14 +91,15 @@
         for kind in range(2)
     )
     for p in range(FAR):
-        out_ref[p] = jnp.where(me < p, kv, qg)
+        out_ref[p] = jnp.where(me < FAR_ORDER[p], kv, qg)
 
 
 def inside_kernel(near_ref, out_ref):
     zero = jnp.zeros(near_ref.shape[2:], f32)
     before, after = zero, zero
     for i in range(NEAR):
-        last = NEAR - 1 - i
+        last = NEAR_AT[NEAR - 1 - i]
+        i = NEAR_AT[i]
         out_ref[i, 0] = before
         out_ref[last, 1] = after
         before = before + near_ref[i, 0].astype(f32)
@@ -97,8 +111,9 @@
     rowidx = lax.broadcasted_iota(jnp.int32, (tokens, tokens), 0)
     colidx = lax.broadcasted_iota(jnp.int32, (tokens, tokens), 1)
     causal = rowidx >= colidx
+    grad = rows_of(grad_ref)
     for h in range(2):
-        q, k, v, g = (r[:, head(h)] for r in (query_ref, key_ref, value_ref, grad_ref))
+        q, k, v, g = (r[:, head(h)] for r in (query_ref, key_ref, value_ref, grad))
         score_go = jnp.where(causal, dot(g, v, 1, 1), 0.0).astype(bf16)
         score_qk = jnp.where(causal, dot(q, k, 1, 1), 0.0).astype(bf16)
         dquery_ref[:, head(h)] = dot(score_go, k, 1, 0)
@@ -112,8 +127,8 @@
     before, after = zero, zero
     for p in range(FAR):
         block = far_ref[p].astype(f32)
-        before = before + jnp.where(p < me, block, zero)
-        after = after + jnp.where(p > me, block, zero)
+        before = before + jnp.where(FAR_ORDER[p] < me, block, zero)
+        after = after + jnp.where(FAR_ORDER[p] > me, block, zero)
     for i in range(NEAR):
         out_ref[i, 0] = (inside_ref[i, 0] + before).astype(bf16)
         out_ref[i, 1] = (inside_ref[i, 1] + after).astype(bf16)
@@ -122,12 +137,13 @@
 def end_kernel(scale, key_ref, value_ref, grad_ref, states_ref, *refs):
     local_refs, out_refs = refs[:3], refs[3:]
     per_head = NEAR // 2
+    grad = rows_of(grad_ref)
     for h in range(2):
         before, after = (
             states_ref[h * per_head : (h + 1) * per_head, kind].reshape(DH, DH)
             for kind in range(2)
         )
-        k, v, g = (r[:, head(h)] for r in (key_ref, value_ref, grad_ref))
+        k, v, g = (r[:, head(h)] for r in (key_ref, value_ref, grad))
         far = (dot(g, before, 1, 1), dot(v, after, 1, 1), dot(k, after, 1, 0))
         for total, local, out in zip(far, local_refs, out_refs):
             out[:, head(h)] = ((total + local[:, head(h)]) * scale).astype(bf16)
@@ -147,19 +163,21 @@
         space=ANY,
         scratch=[pltpu.SemaphoreType.DMA((heads,))],
     )
-    grad = lax.all_to_all(spread, "head", 0, 0, tiled=True).reshape(tokens, width)
+    grad = lax.all_to_all(
+        spread, "head", 0, 0, axis_index_groups=[HEAD_ORDER], tiled=True
+    )
     states = call(
         states_kernel, "states", [((NEAR, 2, rows, DH), bf16)], query, key, value, grad
     )
-    near = lax.all_to_all(states, ("zl", "c"), 0, 0, tiled=True)
+    near = lax.all_to_all(states, "seq", 0, 0, axis_index_groups=NEAR_GROUPS, tiled=True)
     block = call(blocks_kernel, "blocks", [((FAR, rows, DH), bf16)], near)
-    far = lax.all_to_all(block, ("x", "zh"), 0, 0, tiled=True)
+    far = lax.all_to_all(block, "seq", 0, 0, axis_index_groups=FAR_GROUPS, tiled=True)
     inside = call(inside_kernel, "inside", [((NEAR, 2, rows, DH), f32)], near)
     partial = call(
         local_kernel, "local", [((tokens, width), f32)] * 3, query, key, value, grad, flops=200_000_000
     )
     mine = call(prefix_kernel, "prefix", [((NEAR, 2, rows, DH), bf16)], far, inside)
-    ends = lax.all_to_all(mine, ("zl", "c"), 0, 0, tiled=True)
+    ends = lax.all_to_all(mine, "seq", 0, 0, axis_index_groups=NEAR_GROUPS, tiled=True)
     outs = call(
         functools.partial(end_kernel, scale),
         "end",
@@ -174,13 +192,11 @@
 
 
 def solution(mesh):
-    split = Mesh(mesh.devices.reshape(X, ZH, ZL, C, -1), ("x", "zh", "zl", "c", "head"))
-    rows = ("x", "zh", "zl", "c")
-    placed = (P(rows, "head"),) * 3
+    placed = (P("seq", "head"),) * 3
     return jax.shard_map(
         local,
-        mesh=split,
-        in_specs=(*placed, P((*rows, "head"), None)),
+        mesh=mesh,
+        in_specs=(*placed, P(("seq", "head"), None)),
         out_specs=placed,
         check_vma=False,
     )

time: 69.9 us -> 59.5 us (0.85)
  waiting for transfers between devices: 14.4 us -> 7.35 us
  starting transfers between devices: 19.4 us -> 17.3 us
  blocking collectives: 30.5 us -> 29.2 us
    all_to_all x2, waiting for transfers between devices: 14.4 us -> 7.35 us  [the longest x1 4.37 us: local(): lax.all_to_all(block, 'seq', 0, 0, axis_index_groups=FAR_GROUPS, tiled=True)]
    all_to_all x2, starting transfers between devices: 19.4 us -> 17.3 us  [the longest x1 10.8 us: local(): lax.all_to_all(block, 'seq', 0, 0, axis_index_groups=FAR_GROUPS, tiled=True)]
    all_to_all x2, blocking collectives: 30.5 us -> 29.2 us  [the longest x1 17.6 us: local(): lax.all_to_all(states, 'seq', 0, 0, axis_index_groups=NEAR_GROUPS, tiled=...]
where the time goes in v4:
time: 59.5 us; the launch traced here: 59.1 us
  blocking collectives  29.2 us (49%)
  starting transfers between devices  17.3 us (29%)
  waiting for transfers between devices  7.35 us (12%)
  Pallas kernels  3.59 us (6%)
  local copies, waits for them, and re-layouts  0.91 us (2%)
  between operations  0.69 us (1%)
    all_to_all x1, blocking collectives, local(): lax.all_to_all(states, 'seq', 0, 0, axis_index_groups=NEAR_GROUPS, tiled=...  17.6 us
    all_to_all x1, blocking collectives, local(): lax.all_to_all(spread, 'head', 0, 0, axis_index_groups=[HEAD_ORDER], tile...  11.7 us
    all_to_all x1, starting transfers between devices, local(): lax.all_to_all(block, 'seq', 0, 0, axis_index_groups=FAR_GROUPS, tiled=True)  10.8 us
    all_to_all x1, starting transfers between devices, local(): lax.all_to_all(mine, 'seq', 0, 0, axis_index_groups=NEAR_GROUPS, tiled=True)  6.5 us
    all_to_all x1, waiting for transfers between devices, local(): lax.all_to_all(block, 'seq', 0, 0, axis_index_groups=FAR_GROUPS, tiled=True)  4.37 us
    pallas_call x7, Pallas kernels, call(): pl.pallas_call(kernel, out_shape=[jax.ShapeDtypeStruct(shape, dtype) for...  3.59 us
    all_to_all x1, waiting for transfers between devices, local(): lax.all_to_all(mine, 'seq', 0, 0, axis_index_groups=NEAR_GROUPS, tiled=True)  2.98 us
  transfers between devices with their start and end apart: 2, of which 2 were waited for; matrix products, arithmetic and copies ran while one was open for 0% of the time, Pallas kernels for 1%

profile of v4, /device:TPU:1, one launch (start us, length us, event | category | flops | bytes accessed | tf_op | source)
XLA Modules:
  0.0 59.1 jit_solution(5785416312486677990)
XLA Ops:
  0.6 0.0 copy-start.3
  0.6 0.9 %copy-done.3 = bf16[32,2048]{1,0:T(8,128)(2,1)S(1)} copy-done((bf16[32,2048]{1,0:T(8,128)(2,1)S(1)}, bf16[32,2048]{1,0:T(8,128)(2,1)}, u32[]{:S(2)}) %copy-start.3) | copy-done | bytes 131096
  1.5 0.0 copy-start.2
  1.5 0.1 spread.1
  1.7 0.0 copy-start
  1.7 0.0 copy-start.1
  1.7 11.7 %all_to_all.20.grad_ref = bf16[8,32,256]{2,1,0:T(8,128)(2,1)S(1)} all-to-all(bf16[8,32,256]{2,1,0:T(8,128)(2,1)S(1)} %spread.1), channel_id=1, replica_groups={{4,3,5,2,6,1,7,0},{12,11,13,10,14,9,15,8},{20,19,21,18,22,17,23,16},{28..., dimensions={0} | all-to-all | bytes 262144 | tf_op jit(solution)/shard_map/all_to_all | solution.py:166
  13.3 0.0 copy-done.2
  13.3 0.0 copy-done
  13.4 0.0 copy-done.1
  13.4 0.3 states.1
  13.6 17.6 %all_to_all.21.near_ref = bf16[8,2,32,128]{3,2,1,0:T(8,128)(2,1)S(1)} all-to-all(bf16[8,2,32,128]{3,2,1,0:T(8,128)(2,1)S(1)} %states.1), channel_id=1, replica_groups={{56,48,40,32,24,16,8,0},{120,112,104,96,88,80,72,64},{184,176,168,160,1..., dimensions={0} | all-to-all | bytes 262144 | tf_op jit(solution)/shard_map/all_to_all | solution.py:172
  31.2 0.7 %blocks.1 = bf16[12,32,128]{2,1,0:T(8,128)(2,1)} custom-call(bf16[8,2,32,128]{3,2,1,0:T(8,128)(2,1)S(1)} %all_to_all.21.near_ref), custom_call_target="tpu_custom_call" | custom-call | flops 1000000 | bytes 229376 | tf_op jit(solution)/shard_map/blocks/pallas_call | solution.py:32
  31.9 10.8 %all-to-all-start.2 = ((bf16[12,32,128]{2,1,0:T(8,128)(2,1)}), bf16[12,32,128]{2,1,0:T(8,128)(2,1)S(1)}, u32[]{:S(2)}, u32[]{:S(2)}) async-start(bf16[12,32,128]{2,1,0:T(8,128)(2,1)} %blocks.1), calls=%async_computation.2 | async-start | bytes 196608 | tf_op jit(solution)/shard_map/all_to_all | solution.py:174
  42.7 4.4 %all-to-all-done.2.far_ref = bf16[12,32,128]{2,1,0:T(8,128)(2,1)S(1)} async-done(((bf16[12,32,128]{2,1,0:T(8,128)(2,1)}), bf16[12,32,128]{2,1,0:T(8,128)(2,1)S(1)}, u32[]{:S(2)}, u32[]{:S(2)}) %all-to-all-start.2) | async-done | bytes 98336 | tf_op jit(solution)/shard_map/all_to_all | solution.py:174
  47.1 0.7 %prefix.1 = bf16[8,2,32,128]{3,2,1,0:T(8,128)(2,1)} custom-call(bf16[12,32,128]{2,1,0:T(8,128)(2,1)S(1)} %all-to-all-done.2.far_ref, f32[8,2,32,128]{3,2,1,0:T(8,128)S(1)} %inside.1.inside_ref), custom_call_target="tpu_custom_call" | custom-call | flops 1000000 | bytes 491520 | tf_op jit(solution)/shard_map/prefix/pallas_call | solution.py:32
  47.8 6.5 %all-to-all-start.3 = ((bf16[8,2,32,128]{3,2,1,0:T(8,128)(2,1)}), bf16[8,2,32,128]{3,2,1,0:T(8,128)(2,1)S(1)}, u32[]{:S(2)}, u32[]{:S(2)}) async-start(bf16[8,2,32,128]{3,2,1,0:T(8,128)(2,1)} %prefix.1), calls=%async_computation.3 | async-start | bytes 262144 | tf_op jit(solution)/shard_map/all_to_all | solution.py:180
  54.3 0.8 %local.1 = (f32[256,256]{1,0:T(8,128)S(1)}, f32[256,256]{1,0:T(8,128)S(1)}, f32[256,256]{1,0:T(8,128)S(1)}) custom-call(bf16[256,256]{1,0:T(8,128)(2,1)S(1)} %copy-done.2, bf16[256,256]{1,0:T(8,128)(2,1)S(1)} %copy-done, bf16[256,256]{1,0:T(8,128)(2,1)S(1)} %copy-done.1, bf16[8,32,256]{2,1,0:T(8,128)(2,1)S(1)} %all_to_all.20.grad_ref), custom_call_target="tpu_custom_call" | custom-call | flops 200000000 | bytes 1310720 | tf_op jit(solution)/shard_map/local/pallas_call | solution.py:32
  55.1 3.0 %all-to-all-done.3.states_ref = bf16[8,2,32,128]{3,2,1,0:T(8,128)(2,1)S(1)} async-done(((bf16[8,2,32,128]{3,2,1,0:T(8,128)(2,1)}), bf16[8,2,32,128]{3,2,1,0:T(8,128)(2,1)S(1)}, u32[]{:S(2)}, u32[]{:S(2)}) %all-to-all-start.3) | async-done | bytes 131104 | tf_op jit(solution)/shard_map/all_to_all | solution.py:180
  58.1 1.0 %end.1 = (bf16[256,256]{1,0:T(8,128)(2,1)}, bf16[256,256]{1,0:T(8,128)(2,1)}, bf16[256,256]{1,0:T(8,128)(2,1)}) custom-call(bf16[256,256]{1,0:T(8,128)(2,1)S(1)} %copy-done, bf16[256,256]{1,0:T(8,128)(2,1)S(1)} %copy-done.1, bf16[8,32,256]{2,1,0:T(8,128)(2,1)S(1)} %all_to_all.20.grad_ref, bf16[8,2,32,128]{3,2,1,0:T(8,128)(2,1)S(1)} %all-to-all-done.3.states_ref, ...), custom_call_target="tpu_custom_call" | custom-call | flops 1000000 | bytes 1703936 | tf_op jit(solution)/shard_map/end/pallas_call | solution.py:32
  (1 shorter events, 0.0 us)
Async XLA Ops:
  0.6 0.9 %copy-start.3 = (bf16[32,2048]{1,0:T(8,128)(2,1)S(1)}, bf16[32,2048]{1,0:T(8,128)(2,1)}, u32[]{:S(2)}) copy-start(bf16[32,2048]{1,0:T(8,128)(2,1)} %grad_ref.1) | copy-start | bytes 393220
  1.5 11.8 %copy-start.2 = (bf16[256,256]{1,0:T(8,128)(2,1)S(1)}, bf16[256,256]{1,0:T(8,128)(2,1)}, u32[]{:S(2)}) copy-start(bf16[256,256]{1,0:T(8,128)(2,1)} %query_ref.3) | copy-start | bytes 393220
  1.7 11.7 %copy-start = (bf16[256,256]{1,0:T(8,128)(2,1)S(1)}, bf16[256,256]{1,0:T(8,128)(2,1)}, u32[]{:S(2)}) copy-start(bf16[256,256]{1,0:T(8,128)(2,1)} %key_ref.5) | copy-start | bytes 393220
  1.7 11.7 %copy-start.1 = (bf16[256,256]{1,0:T(8,128)(2,1)S(1)}, bf16[256,256]{1,0:T(8,128)(2,1)}, u32[]{:S(2)}) copy-start(bf16[256,256]{1,0:T(8,128)(2,1)} %value_ref.5) | copy-start | bytes 393220
  31.9 15.2 %all-to-all-start.2 = ((bf16[12,32,128]{2,1,0:T(8,128)(2,1)}), bf16[12,32,128]{2,1,0:T(8,128)(2,1)S(1)}, u32[]{:S(2)}, u32[]{:S(2)}) async-start(bf16[12,32,128]{2,1,0:T(8,128)(2,1)} %blocks.1), calls=%async_computation.2 | async-start | bytes 196608 | tf_op jit(solution)/shard_map/all_to_all | solution.py:174
  47.8 10.3 %all-to-all-start.3 = ((bf16[8,2,32,128]{3,2,1,0:T(8,128)(2,1)}), bf16[8,2,32,128]{3,2,1,0:T(8,128)(2,1)S(1)}, u32[]{:S(2)}, u32[]{:S(2)}) async-start(bf16[8,2,32,128]{3,2,1,0:T(8,128)(2,1)} %prefix.1), calls=%async_computation.3 | async-start | bytes 262144 | tf_op jit(solution)/shard_map/all_to_all | solution.py:180

commit v5 on v4

v5 whole, which is shorter than its diff:
```python
import functools
import math

import jax
import jax.numpy as jnp
from jax import lax
from jax.experimental import pallas as pl
from jax.experimental.pallas import tpu as pltpu
from jax.sharding import Mesh
from jax.sharding import PartitionSpec as P

DH = 128
X, ZH, ZL, C = 4, 3, 4, 2
NEAR, FAR = ZL * C, X * ZH
ROOM = 8 << 20
NEAR_ORDER = [7, 6, 5, 4, 3, 2, 1, 0]
FAR_ORDER = [8, 11, 10, 9, 7, 6, 5, 4, 3, 2, 1, 0]
HEAD_ORDER = [5, 4, 6, 3, 7, 2, 1, 0]
HEADS = len(HEAD_ORDER)
HEAD_AT = [HEAD_ORDER.index(i) for i in range(HEADS)]
BACK_ORDER = [5, 7, 6, 4, 3, 2, 1, 0]
BACK_AT = [BACK_ORDER.index(i) for i in range(NEAR)]
BACK_GROUPS = [[(f * NEAR) + i for i in BACK_ORDER] for f in range(FAR)]
NEAR_AT = [NEAR_ORDER.index(i) for i in range(NEAR)]
NEAR_GROUPS = [[(f * NEAR) + i for i in NEAR_ORDER] for f in range(FAR)]
FAR_GROUPS = [[f * NEAR + i for f in FAR_ORDER] for i in range(NEAR)]
f32, bf16 = jnp.float32, jnp.bfloat16
VMEM = pl.BlockSpec(memory_space=pltpu.VMEM)
ANY = pl.BlockSpec(memory_space=pl.ANY)


def call(kernel, name, outs, *args, space=VMEM, out_space=None, flops=1_000_000, scratch=()):
    moved = sum(a.size * a.dtype.itemsize for a in args)
    moved += sum(math.prod(shape) * jnp.dtype(dtype).itemsize for shape, dtype in outs)
    out = pl.pallas_call(
        kernel,
        out_shape=[jax.ShapeDtypeStruct(shape, dtype) for shape, dtype in outs],
        in_specs=[space] * len(args),
        out_specs=[out_space or space] * len(outs),
        scratch_shapes=scratch,
        compiler_params=pltpu.CompilerParams(vmem_limit_bytes=ROOM),
        cost_estimate=pl.CostEstimate(flops=flops, bytes_accessed=moved, transcendentals=0),
        name=name,
    )(*args)
    return out[0] if len(outs) == 1 else out


def dot(a, b, over_a, over_b):
    return lax.dot_general(a, b, (((over_a,), (over_b,)), ((), ())), preferred_element_type=f32)


def head(h):
    return slice(h * DH, (h + 1) * DH)


def rows_of(grad_ref):
    return jnp.concatenate([grad_ref[HEAD_AT[t]] for t in range(HEADS)], axis=0)


def block_index():
    return lax.axis_index("seq") // NEAR


def spread_kernel(grad_ref, out_ref, sems):
    parts, _, width = out_ref.shape
    copies = [
        pltpu.make_async_copy(
            grad_ref.at[:, j * width : (j + 1) * width], out_ref.at[HEAD_AT[j]], sems.at[j]
        )
        for j in range(parts)
    ]
    for copy in copies:
        copy.start()
    for copy in copies:
        copy.wait()


def states_kernel(query_ref, key_ref, value_ref, grad_ref, out_ref):
    per_head, rows = NEAR // 2, 2 * DH // NEAR
    grad = rows_of(grad_ref)
    for h in range(2):
        kv = dot(key_ref[:, head(h)], value_ref[:, head(h)], 0, 0)
        qg = dot(query_ref[:, head(h)], grad[:, head(h)], 0, 0)
        for kind, state in enumerate((kv, qg)):
            state = state.astype(out_ref.dtype)
            for j in range(per_head):
                out_ref[NEAR_AT[h * per_head + j], kind] = state[j * rows : (j + 1) * rows]


def blocks_kernel(near_ref, out_ref):
    me = block_index()
    kv, qg = (
        sum(near_ref[i, kind].astype(f32) for i in range(NEAR)).astype(out_ref.dtype)
        for kind in range(2)
    )
    for p in range(FAR):
        out_ref[p] = jnp.where(me < FAR_ORDER[p], kv, qg)


def prefix_kernel(far_ref, near_ref, out_ref):
    me = block_index()
    zero = jnp.zeros(far_ref.shape[1:], f32)
    before, after = zero, zero
    for p in range(FAR):
        block = far_ref[p].astype(f32)
        before = before + jnp.where(FAR_ORDER[p] < me, block, zero)
        after = after + jnp.where(FAR_ORDER[p] > me, block, zero)
    for i in range(NEAR):
        last = NEAR - 1 - i
        out_ref[BACK_AT[i], 0] = before.astype(bf16)
        out_ref[BACK_AT[last], 1] = after.astype(bf16)
        before = before + near_ref[NEAR_AT[i], 0].astype(f32)
        after = after + near_ref[NEAR_AT[last], 1].astype(f32)


def end_kernel(scale, query_ref, key_ref, value_ref, grad_ref, states_ref, *refs):
    out_refs = refs
    per_head = NEAR // 2
    tokens = query_ref.shape[0]
    rowidx = lax.broadcasted_iota(jnp.int32, (tokens, tokens), 0)
    colidx = lax.broadcasted_iota(jnp.int32, (tokens, tokens), 1)
    causal, causal_to = rowidx >= colidx, rowidx <= colidx
    grad = rows_of(grad_ref)

    def finish(which, h, total):
        out_refs[which][:, head(h)] = (total * scale).astype(bf16)

    for h in range(2):
        before, after = (
            jnp.concatenate(
                [states_ref[BACK_AT[h * per_head + j], kind] for j in range(per_head)], axis=0
            )
            for kind in range(2)
        )
        q, k, v, g = (r[:, head(h)] for r in (query_ref, key_ref, value_ref, grad))
        score_qk = jnp.where(causal_to, dot(k, q, 1, 1), 0.0).astype(bf16)
        finish(2, h, dot(score_qk, g, 1, 0) + dot(k, after, 1, 0))
        score_to = jnp.where(causal_to, dot(v, g, 1, 1), 0.0).astype(bf16)
        finish(1, h, dot(score_to, q, 1, 0) + dot(v, after, 1, 1))
        score_go = jnp.where(causal, dot(g, v, 1, 1), 0.0).astype(bf16)
        finish(0, h, dot(score_go, k, 1, 0) + dot(g, before, 1, 1))


def local(query, key, value, grad_out):
    tokens, width = query.shape
    heads = grad_out.shape[1] // width
    rows = 2 * DH // NEAR
    scale = 1.0 / math.sqrt(DH * tokens * X * ZH * ZL * C)

    spread = call(
        spread_kernel,
        "spread",
        [((heads, tokens // heads, width), bf16)],
        grad_out,
        space=ANY,
        scratch=[pltpu.SemaphoreType.DMA((heads,))],
    )
    grad = lax.all_to_all(
        spread, "head", 0, 0, axis_index_groups=[HEAD_ORDER], tiled=True
    )
    states = call(
        states_kernel, "states", [((NEAR, 2, rows, DH), bf16)], query, key, value, grad
    )
    near = lax.all_to_all(states, "seq", 0, 0, axis_index_groups=NEAR_GROUPS, tiled=True)

    block = call(blocks_kernel, "blocks", [((FAR, rows, DH), bf16)], near)
    far = lax.all_to_all(block, "seq", 0, 0, axis_index_groups=FAR_GROUPS, tiled=True)
    mine = call(prefix_kernel, "prefix", [((NEAR, 2, rows, DH), bf16)], far, near)
    ends = lax.all_to_all(mine, "seq", 0, 0, axis_index_groups=BACK_GROUPS, tiled=True)
    outs = call(
        functools.partial(end_kernel, scale),
        "end",
        [((tokens, width), bf16)] * 3,
        query,
        key,
        value,
        grad,
        ends,
        flops=218_000_000,
    )
    return tuple(outs)


def solution(mesh):
    placed = (P("seq", "head"),) * 3
    return jax.shard_map(
        local,
        mesh=mesh,
        in_specs=(*placed, P(("seq", "head"), None)),
        out_specs=placed,
        check_vma=False,
    )
```

time: 59.5 us -> 58.2 us (0.978)
  blocking collectives: 29.2 us -> 54.2 us
  starting transfers between devices: 17.3 us -> 0 us
  waiting for transfers between devices: 7.35 us -> 0 us
  Pallas kernels: 3.59 us -> 2.06 us
    all_to_all x0 -> x2, blocking collectives: none -> 25 us  [the longest x1 14.9 us: local(): lax.all_to_all(block, 'seq', 0, 0, axis_index_groups=FAR_GROUPS, tiled=True)]
    all_to_all x2 -> x0, starting transfers between devices: 17.3 us -> none  [the longest x1 10.8 us: local(): lax.all_to_all(block, 'seq', 0, 0, axis_index_groups=FAR_GROUPS, tiled=True)]
    all_to_all x2 -> x0, waiting for transfers between devices: 7.35 us -> none  [the longest x1 4.37 us: local(): lax.all_to_all(block, 'seq', 0, 0, axis_index_groups=FAR_GROUPS, tiled=True)]
    pallas_call x7 -> x5, Pallas kernels: 3.59 us -> 2.06 us  [call(): pl.pallas_call(kernel, out_shape=[jax.ShapeDtypeStruct(shape, dtype) for...]
  transfers between devices with their start and end apart: 2 -> 0, of which waited for: 2 -> 0; matrix products, arithmetic and copies ran while one was open for 0% -> 0% of each run, Pallas kernels for 1% -> 0%
where the time goes in v5:
time: 58.2 us; the launch traced here: 57.9 us
  blocking collectives  54.2 us (93%)
  Pallas kernels  2.06 us (4%)
  local copies, waits for them, and re-layouts  0.91 us (2%)
  between operations  0.69 us (1%)
    all_to_all x1, blocking collectives, local(): lax.all_to_all(states, 'seq', 0, 0, axis_index_groups=NEAR_GROUPS, tiled=...  17.4 us
    all_to_all x1, blocking collectives, local(): lax.all_to_all(block, 'seq', 0, 0, axis_index_groups=FAR_GROUPS, tiled=True)  14.9 us
    all_to_all x1, blocking collectives, local(): lax.all_to_all(spread, 'head', 0, 0, axis_index_groups=[HEAD_ORDER], tile...  11.8 us
    all_to_all x1, blocking collectives, local(): lax.all_to_all(mine, 'seq', 0, 0, axis_index_groups=BACK_GROUPS, tiled=True)  10.1 us
    pallas_call x5, Pallas kernels, call(): pl.pallas_call(kernel, out_shape=[jax.ShapeDtypeStruct(shape, dtype) for...  2.06 us

profile of v5, /device:TPU:1, one launch (start us, length us, event | category | flops | bytes accessed | tf_op | source)
XLA Modules:
  0.0 57.9 jit_solution(15974511906096080063)
XLA Ops:
  0.6 0.0 copy-start.3
  0.6 0.9 %copy-done.3 = bf16[32,2048]{1,0:T(8,128)(2,1)S(1)} copy-done((bf16[32,2048]{1,0:T(8,128)(2,1)S(1)}, bf16[32,2048]{1,0:T(8,128)(2,1)}, u32[]{:S(2)}) %copy-start.3) | copy-done | bytes 131096
  1.5 0.0 copy-start.2
  1.5 0.1 spread.1
  1.7 0.0 copy-start
  1.7 0.0 copy-start.1
  1.7 11.8 %all_to_all.20.grad_ref = bf16[8,32,256]{2,1,0:T(8,128)(2,1)S(1)} all-to-all(bf16[8,32,256]{2,1,0:T(8,128)(2,1)S(1)} %spread.1), channel_id=1, replica_groups={{5,4,6,3,7,2,1,0},{13,12,14,11,15,10,9,8},{21,20,22,19,23,18,17,16},{29..., dimensions={0} | all-to-all | bytes 262144 | tf_op jit(solution)/shard_map/all_to_all | solution.py:158
  13.5 0.0 copy-done.2
  13.5 0.0 copy-done
  13.5 0.0 copy-done.1
  13.5 0.3 states.1
  13.8 17.4 %all_to_all.21.near_ref = bf16[8,2,32,128]{3,2,1,0:T(8,128)(2,1)S(1)} all-to-all(bf16[8,2,32,128]{3,2,1,0:T(8,128)(2,1)S(1)} %states.1), channel_id=1, replica_groups={{56,48,40,32,24,16,8,0},{120,112,104,96,88,80,72,64},{184,176,168,160,1..., dimensions={0} | all-to-all | bytes 262144 | tf_op jit(solution)/shard_map/all_to_all | solution.py:164
  31.2 14.9 %all_to_all.22.far_ref = bf16[12,32,128]{2,1,0:T(8,128)(2,1)S(1)} all-to-all(bf16[12,32,128]{2,1,0:T(8,128)(2,1)S(1)} %blocks.1), channel_id=1, replica_groups={{512,704,640,576,448,384,320,256,192,128,64,0},{520,712,648,584,456,392..., dimensions={0} | all-to-all | bytes 196608 | tf_op jit(solution)/shard_map/all_to_all | solution.py:167
  46.2 0.1 prefix.1
  46.3 10.1 %all_to_all.23.states_ref = bf16[8,2,32,128]{3,2,1,0:T(8,128)(2,1)S(1)} all-to-all(bf16[8,2,32,128]{3,2,1,0:T(8,128)(2,1)S(1)} %prefix.1), channel_id=1, replica_groups={{40,56,48,32,24,16,8,0},{104,120,112,96,88,80,72,64},{168,184,176,160,1..., dimensions={0} | all-to-all | bytes 262144 | tf_op jit(solution)/shard_map/all_to_all | solution.py:169
  56.4 1.6 %end.1 = (bf16[256,256]{1,0:T(8,128)(2,1)}, bf16[256,256]{1,0:T(8,128)(2,1)}, bf16[256,256]{1,0:T(8,128)(2,1)}) custom-call(bf16[256,256]{1,0:T(8,128)(2,1)S(1)} %copy-done, bf16[256,256]{1,0:T(8,128)(2,1)S(1)} %copy-done.1, bf16[256,256]{1,0:T(8,128)(2,1)S(1)} %copy-done.2, bf16[8,32,256]{2,1,0:T(8,128)(2,1)S(1)} %all_to_all.20.grad_ref, ...), custom_call_target="tpu_custom_call" | custom-call | flops 218000000 | bytes 1048576 | tf_op jit(solution)/shard_map/end/pallas_call | solution.py:35
  (1 shorter events, 0.0 us)
Async XLA Ops:
  0.6 0.9 %copy-start.3 = (bf16[32,2048]{1,0:T(8,128)(2,1)S(1)}, bf16[32,2048]{1,0:T(8,128)(2,1)}, u32[]{:S(2)}) copy-start(bf16[32,2048]{1,0:T(8,128)(2,1)} %grad_ref.1) | copy-start | bytes 393220
  1.5 11.9 %copy-start.2 = (bf16[256,256]{1,0:T(8,128)(2,1)S(1)}, bf16[256,256]{1,0:T(8,128)(2,1)}, u32[]{:S(2)}) copy-start(bf16[256,256]{1,0:T(8,128)(2,1)} %value_ref.3) | copy-start | bytes 393220
  1.7 11.8 %copy-start = (bf16[256,256]{1,0:T(8,128)(2,1)S(1)}, bf16[256,256]{1,0:T(8,128)(2,1)}, u32[]{:S(2)}) copy-start(bf16[256,256]{1,0:T(8,128)(2,1)} %query_ref.3) | copy-start | bytes 393220
  1.7 11.8 %copy-start.1 = (bf16[256,256]{1,0:T(8,128)(2,1)S(1)}, bf16[256,256]{1,0:T(8,128)(2,1)}, u32[]{:S(2)}) copy-start(bf16[256,256]{1,0:T(8,128)(2,1)} %key_ref.3) | copy-start | bytes 393220

commit v6 on v5

--- a/solution.py
+++ b/solution.py
@@ -87,7 +87,31 @@
                 out_ref[NEAR_AT[h * per_head + j], kind] = state[j * rows : (j + 1) * rows]
 
 
-def blocks_kernel(near_ref, out_ref):
+def early():
+    return lax.rem(block_index(), ZH) == 0
+
+
+def local_products(query_ref, key_ref, value_ref, grad_ref):
+    tokens = query_ref.shape[0]
+    rowidx = lax.broadcasted_iota(jnp.int32, (tokens, tokens), 0)
+    colidx = lax.broadcasted_iota(jnp.int32, (tokens, tokens), 1)
+    causal, causal_to = rowidx >= colidx, rowidx <= colidx
+    grad = rows_of(grad_ref)
+    parts, scores = [], []
+    for h in range(2):
+        q, k, v, g = (r[:, head(h)] for r in (query_ref, key_ref, value_ref, grad))
+        parts.append((q, k, g))
+        scores.append((dot(g, v, 1, 1), dot(v, g, 1, 1), dot(k, q, 1, 1)))
+    products = []
+    for (q, k, g), (go, go_to, qk_to) in zip(parts, scores):
+        go = jnp.where(causal, go, 0.0).astype(bf16)
+        go_to = jnp.where(causal_to, go_to, 0.0).astype(bf16)
+        qk_to = jnp.where(causal_to, qk_to, 0.0).astype(bf16)
+        products.append((dot(go, k, 1, 0), dot(go_to, q, 1, 0), dot(qk_to, g, 1, 0)))
+    return products
+
+
+def blocks_kernel(near_ref, query_ref, key_ref, value_ref, grad_ref, out_ref, *local_refs):
     me = block_index()
     kv, qg = (
         sum(near_ref[i, kind].astype(f32) for i in range(NEAR)).astype(out_ref.dtype)
@@ -95,6 +119,13 @@
     )
     for p in range(FAR):
         out_ref[p] = jnp.where(me < FAR_ORDER[p], kv, qg)
+
+    @pl.when(early())
+    def _():
+        products = local_products(query_ref, key_ref, value_ref, grad_ref)
+        for h in range(2):
+            for product, local in zip(products[h], local_refs):
+                local[:, head(h)] = product
 
 
 def prefix_kernel(far_ref, near_ref, out_ref):
@@ -114,31 +145,31 @@
 
 
 def end_kernel(scale, query_ref, key_ref, value_ref, grad_ref, states_ref, *refs):
-    out_refs = refs
+    local_refs, out_refs = refs[:3], refs[3:]
     per_head = NEAR // 2
-    tokens = query_ref.shape[0]
-    rowidx = lax.broadcasted_iota(jnp.int32, (tokens, tokens), 0)
-    colidx = lax.broadcasted_iota(jnp.int32, (tokens, tokens), 1)
-    causal, causal_to = rowidx >= colidx, rowidx <= colidx
-    grad = rows_of(grad_ref)
-
-    def finish(which, h, total):
-        out_refs[which][:, head(h)] = (total * scale).astype(bf16)
-
-    for h in range(2):
-        before, after = (
-            jnp.concatenate(
-                [states_ref[BACK_AT[h * per_head + j], kind] for j in range(per_head)], axis=0
+
+    def finish(locals_of):
+        grad = rows_of(grad_ref)
+        for h in range(2):
+            before, after = (
+                jnp.concatenate(
+                    [states_ref[BACK_AT[h * per_head + j], kind] for j in range(per_head)], axis=0
+                )
+                for kind in range(2)
             )
-            for kind in range(2)
-        )
-        q, k, v, g = (r[:, head(h)] for r in (query_ref, key_ref, value_ref, grad))
-        score_qk = jnp.where(causal_to, dot(k, q, 1, 1), 0.0).astype(bf16)
-        finish(2, h, dot(score_qk, g, 1, 0) + dot(k, after, 1, 0))
-        score_to = jnp.where(causal_to, dot(v, g, 1, 1), 0.0).astype(bf16)
-        finish(1, h, dot(score_to, q, 1, 0) + dot(v, after, 1, 1))
-        score_go = jnp.where(causal, dot(g, v, 1, 1), 0.0).astype(bf16)
-        finish(0, h, dot(score_go, k, 1, 0) + dot(g, before, 1, 1))
+            k, v, g = (r[:, head(h)] for r in (key_ref, value_ref, grad))
+            far = (dot(g, before, 1, 1), dot(v, after, 1, 1), dot(k, after, 1, 0))
+            for total, local, out in zip(far, locals_of(h), out_refs):
+                out[:, head(h)] = ((total + local) * scale).astype(bf16)
+
+    @pl.when(early())
+    def _():
+        finish(lambda h: [local[:, head(h)] for local in local_refs])
+
+    @pl.when(jnp.logical_not(early()))
+    def _():
+        products = local_products(query_ref, key_ref, value_ref, grad_ref)
+        finish(lambda h: products[h])
 
 
 def local(query, key, value, grad_out):
@@ -163,7 +194,17 @@
     )
     near = lax.all_to_all(states, "seq", 0, 0, axis_index_groups=NEAR_GROUPS, tiled=True)
 
-    block = call(blocks_kernel, "blocks", [((FAR, rows, DH), bf16)], near)
+    block, *partial = call(
+        blocks_kernel,
+        "blocks",
+        [((FAR, rows, DH), bf16)] + [((tokens, width), f32)] * 3,
+        near,
+        query,
+        key,
+        value,
+        grad,
+        flops=168_000_000,
+    )
     far = lax.all_to_all(block, "seq", 0, 0, axis_index_groups=FAR_GROUPS, tiled=True)
     mine = call(prefix_kernel, "prefix", [((NEAR, 2, rows, DH), bf16)], far, near)
     ends = lax.all_to_all(mine, "seq", 0, 0, axis_index_groups=BACK_GROUPS, tiled=True)
@@ -176,6 +217,7 @@
         value,
         grad,
         ends,
+        *partial,
         flops=218_000_000,
     )
     return tuple(outs)

time: 58.2 us -> 57.6 us (0.990)
  no operation moved by 1% of the time
where the time goes in v6:
time: 57.6 us; the launch traced here: 57.4 us
  blocking collectives  53.7 us (93%)
  Pallas kernels  2.09 us (4%)
  local copies, waits for them, and re-layouts  0.91 us (2%)
  between operations  0.69 us (1%)
    all_to_all x1, blocking collectives, local(): lax.all_to_all(states, 'seq', 0, 0, axis_index_groups=NEAR_GROUPS, tiled=...  17.4 us
    all_to_all x1, blocking collectives, local(): lax.all_to_all(block, 'seq', 0, 0, axis_index_groups=FAR_GROUPS, tiled=True)  14.4 us
    all_to_all x1, blocking collectives, local(): lax.all_to_all(spread, 'head', 0, 0, axis_index_groups=[HEAD_ORDER], tile...  11.8 us
    all_to_all x1, blocking collectives, local(): lax.all_to_all(mine, 'seq', 0, 0, axis_index_groups=BACK_GROUPS, tiled=True)  10.1 us
    pallas_call x5, Pallas kernels, call(): pl.pallas_call(kernel, out_shape=[jax.ShapeDtypeStruct(shape, dtype) for...  2.09 us

profile of v6, /device:TPU:1, one launch (start us, length us, event | category | flops | bytes accessed | tf_op | source)
XLA Modules:
  0.0 57.4 jit_solution(13142385778149447696)
XLA Ops:
  0.6 0.0 copy-start.3
  0.6 0.9 %copy-done.3 = bf16[32,2048]{1,0:T(8,128)(2,1)S(1)} copy-done((bf16[32,2048]{1,0:T(8,128)(2,1)S(1)}, bf16[32,2048]{1,0:T(8,128)(2,1)}, u32[]{:S(2)}) %copy-start.3) | copy-done | bytes 131096
  1.5 0.0 copy-start.2
  1.5 0.1 spread.1
  1.7 0.0 copy-start
  1.7 0.0 copy-start.1
  1.7 11.8 %all_to_all.20.grad_ref = bf16[8,32,256]{2,1,0:T(8,128)(2,1)S(1)} all-to-all(bf16[8,32,256]{2,1,0:T(8,128)(2,1)S(1)} %spread.1), channel_id=1, replica_groups={{5,4,6,3,7,2,1,0},{13,12,14,11,15,10,9,8},{21,20,22,19,23,18,17,16},{29..., dimensions={0} | all-to-all | bytes 262144 | tf_op jit(solution)/shard_map/all_to_all | solution.py:189
  13.5 0.0 copy-done.2
  13.5 0.0 copy-done
  13.5 0.0 copy-done.1
  13.5 0.3 states.1
  13.8 17.4 %all_to_all.21.near_ref = bf16[8,2,32,128]{3,2,1,0:T(8,128)(2,1)S(1)} all-to-all(bf16[8,2,32,128]{3,2,1,0:T(8,128)(2,1)S(1)} %states.1), channel_id=1, replica_groups={{56,48,40,32,24,16,8,0},{120,112,104,96,88,80,72,64},{184,176,168,160,1..., dimensions={0} | all-to-all | bytes 262144 | tf_op jit(solution)/shard_map/all_to_all | solution.py:195
  31.2 0.6 %blocks.1 = (bf16[12,32,128]{2,1,0:T(8,128)(2,1)S(1)}, f32[256,256]{1,0:T(8,128)S(1)}, f32[256,256]{1,0:T(8,128)S(1)}, f32[256,256]{1,0:T(8,128)S(1)}) custom-call(bf16[8,2,32,128]{3,2,1,0:T(8,128)(2,1)S(1)} %all_to_all.21.near_ref, bf16[256,256]{1,0:T(8,128)(2,1)S(1)} %copy-done, bf16[256,256]{1,0:T(8,128)(2,1)S(1)} %copy-done.1, ...), custom_call_target="tpu_custom_call" | custom-call | flops 168000000 | bytes 1540096 | tf_op jit(solution)/shard_map/blocks/pallas_call | solution.py:35
  31.8 14.4 %all_to_all.22.far_ref = bf16[12,32,128]{2,1,0:T(8,128)(2,1)S(1)} all-to-all(bf16[12,32,128]{2,1,0:T(8,128)(2,1)S(1)} %get-tuple-element.7), channel_id=1, replica_groups={{512,704,640,576,448,384,320,256,192,128,64,0},{520,712,648,584,456,392..., dimensions={0} | all-to-all | bytes 196608 | tf_op jit(solution)/shard_map/all_to_all | solution.py:208
  46.2 0.1 prefix.1
  46.3 10.1 %all_to_all.23.states_ref = bf16[8,2,32,128]{3,2,1,0:T(8,128)(2,1)S(1)} all-to-all(bf16[8,2,32,128]{3,2,1,0:T(8,128)(2,1)S(1)} %prefix.1), channel_id=1, replica_groups={{40,56,48,32,24,16,8,0},{104,120,112,96,88,80,72,64},{168,184,176,160,1..., dimensions={0} | all-to-all | bytes 262144 | tf_op jit(solution)/shard_map/all_to_all | solution.py:210
  56.4 1.0 %end.1 = (bf16[256,256]{1,0:T(8,128)(2,1)}, bf16[256,256]{1,0:T(8,128)(2,1)}, bf16[256,256]{1,0:T(8,128)(2,1)}) custom-call(bf16[256,256]{1,0:T(8,128)(2,1)S(1)} %copy-done, bf16[256,256]{1,0:T(8,128)(2,1)S(1)} %copy-done.1, bf16[256,256]{1,0:T(8,128)(2,1)S(1)} %copy-done.2, bf16[8,32,256]{2,1,0:T(8,128)(2,1)S(1)} %all_to_all.20.grad_ref, ...), custom_call_target="tpu_custom_call" | custom-call | flops 218000000 | bytes 1835008 | tf_op jit(solution)/shard_map/end/pallas_call | solution.py:35
Async XLA Ops:
  0.6 0.9 %copy-start.3 = (bf16[32,2048]{1,0:T(8,128)(2,1)S(1)}, bf16[32,2048]{1,0:T(8,128)(2,1)}, u32[]{:S(2)}) copy-start(bf16[32,2048]{1,0:T(8,128)(2,1)} %grad_ref.1) | copy-start | bytes 393220
  1.5 11.9 %copy-start.2 = (bf16[256,256]{1,0:T(8,128)(2,1)S(1)}, bf16[256,256]{1,0:T(8,128)(2,1)}, u32[]{:S(2)}) copy-start(bf16[256,256]{1,0:T(8,128)(2,1)} %value_ref.5) | copy-start | bytes 393220
  1.7 11.8 %copy-start = (bf16[256,256]{1,0:T(8,128)(2,1)S(1)}, bf16[256,256]{1,0:T(8,128)(2,1)}, u32[]{:S(2)}) copy-start(bf16[256,256]{1,0:T(8,128)(2,1)} %query_ref.5) | copy-start | bytes 393220
  1.7 11.8 %copy-start.1 = (bf16[256,256]{1,0:T(8,128)(2,1)S(1)}, bf16[256,256]{1,0:T(8,128)(2,1)}, u32[]{:S(2)}) copy-start(bf16[256,256]{1,0:T(8,128)(2,1)} %key_ref.5) | copy-start | bytes 393220

commit v7 on v6

--- a/solution.py
+++ b/solution.py
@@ -15,7 +15,7 @@
 ROOM = 8 << 20
 NEAR_ORDER = [7, 6, 5, 4, 3, 2, 1, 0]
 FAR_ORDER = [8, 11, 10, 9, 7, 6, 5, 4, 3, 2, 1, 0]
-HEAD_ORDER = [5, 4, 6, 3, 7, 2, 1, 0]
+HEAD_ORDER = [4, 7, 6, 5, 3, 2, 1, 0]
 HEADS = len(HEAD_ORDER)
 HEAD_AT = [HEAD_ORDER.index(i) for i in range(HEADS)]
 BACK_ORDER = [5, 7, 6, 4, 3, 2, 1, 0]

time: 57.6 us -> 57 us (0.990)
  blocking collectives: 53.7 us -> 53 us
where the time goes in v7:
time: 57 us; the launch traced here: 56.7 us
  blocking collectives  53 us (93%)
  Pallas kernels  2.09 us (4%)
  local copies, waits for them, and re-layouts  0.91 us (2%)
  between operations  0.69 us (1%)
    all_to_all x1, blocking collectives, local(): lax.all_to_all(states, 'seq', 0, 0, axis_index_groups=NEAR_GROUPS, tiled=...  17.7 us
    all_to_all x1, blocking collectives, local(): lax.all_to_all(block, 'seq', 0, 0, axis_index_groups=FAR_GROUPS, tiled=True)  13.9 us
    all_to_all x1, blocking collectives, local(): lax.all_to_all(spread, 'head', 0, 0, axis_index_groups=[HEAD_ORDER], tile...  11.4 us
    all_to_all x1, blocking collectives, local(): lax.all_to_all(mine, 'seq', 0, 0, axis_index_groups=BACK_GROUPS, tiled=True)  10 us
    pallas_call x5, Pallas kernels, call(): pl.pallas_call(kernel, out_shape=[jax.ShapeDtypeStruct(shape, dtype) for...  2.09 us

profile of v7, /device:TPU:1, one launch (start us, length us, event | category | flops | bytes accessed | tf_op | source)
XLA Modules:
  0.0 56.7 jit_solution(16859827368889891312)
XLA Ops:
  0.6 0.0 copy-start.3
  0.6 0.9 %copy-done.3 = bf16[32,2048]{1,0:T(8,128)(2,1)S(1)} copy-done((bf16[32,2048]{1,0:T(8,128)(2,1)S(1)}, bf16[32,2048]{1,0:T(8,128)(2,1)}, u32[]{:S(2)}) %copy-start.3) | copy-done | bytes 131096
  1.5 0.0 copy-start.2
  1.5 0.1 spread.1
  1.7 0.0 copy-start
  1.7 0.0 copy-start.1
  1.7 11.4 %all_to_all.20.grad_ref = bf16[8,32,256]{2,1,0:T(8,128)(2,1)S(1)} all-to-all(bf16[8,32,256]{2,1,0:T(8,128)(2,1)S(1)} %spread.1), channel_id=1, replica_groups={{4,7,6,5,3,2,1,0},{12,15,14,13,11,10,9,8},{20,23,22,21,19,18,17,16},{28..., dimensions={0} | all-to-all | bytes 262144 | tf_op jit(solution)/shard_map/all_to_all | solution.py:189
  13.1 0.0 copy-done.2
  13.1 0.0 copy-done
  13.1 0.0 copy-done.1
  13.1 0.3 states.1
  13.4 17.7 %all_to_all.21.near_ref = bf16[8,2,32,128]{3,2,1,0:T(8,128)(2,1)S(1)} all-to-all(bf16[8,2,32,128]{3,2,1,0:T(8,128)(2,1)S(1)} %states.1), channel_id=1, replica_groups={{56,48,40,32,24,16,8,0},{120,112,104,96,88,80,72,64},{184,176,168,160,1..., dimensions={0} | all-to-all | bytes 262144 | tf_op jit(solution)/shard_map/all_to_all | solution.py:195
  31.1 0.6 %blocks.1 = (bf16[12,32,128]{2,1,0:T(8,128)(2,1)S(1)}, f32[256,256]{1,0:T(8,128)S(1)}, f32[256,256]{1,0:T(8,128)S(1)}, f32[256,256]{1,0:T(8,128)S(1)}) custom-call(bf16[8,2,32,128]{3,2,1,0:T(8,128)(2,1)S(1)} %all_to_all.21.near_ref, bf16[256,256]{1,0:T(8,128)(2,1)S(1)} %copy-done, bf16[256,256]{1,0:T(8,128)(2,1)S(1)} %copy-done.1, ...), custom_call_target="tpu_custom_call" | custom-call | flops 168000000 | bytes 1540096 | tf_op jit(solution)/shard_map/blocks/pallas_call | solution.py:35
  31.7 13.9 %all_to_all.22.far_ref = bf16[12,32,128]{2,1,0:T(8,128)(2,1)S(1)} all-to-all(bf16[12,32,128]{2,1,0:T(8,128)(2,1)S(1)} %get-tuple-element.7), channel_id=1, replica_groups={{512,704,640,576,448,384,320,256,192,128,64,0},{520,712,648,584,456,392..., dimensions={0} | all-to-all | bytes 196608 | tf_op jit(solution)/shard_map/all_to_all | solution.py:208
  45.6 0.1 prefix.1
  45.7 10.0 %all_to_all.23.states_ref = bf16[8,2,32,128]{3,2,1,0:T(8,128)(2,1)S(1)} all-to-all(bf16[8,2,32,128]{3,2,1,0:T(8,128)(2,1)S(1)} %prefix.1), channel_id=1, replica_groups={{40,56,48,32,24,16,8,0},{104,120,112,96,88,80,72,64},{168,184,176,160,1..., dimensions={0} | all-to-all | bytes 262144 | tf_op jit(solution)/shard_map/all_to_all | solution.py:210
  55.7 1.0 %end.1 = (bf16[256,256]{1,0:T(8,128)(2,1)}, bf16[256,256]{1,0:T(8,128)(2,1)}, bf16[256,256]{1,0:T(8,128)(2,1)}) custom-call(bf16[256,256]{1,0:T(8,128)(2,1)S(1)} %copy-done, bf16[256,256]{1,0:T(8,128)(2,1)S(1)} %copy-done.1, bf16[256,256]{1,0:T(8,128)(2,1)S(1)} %copy-done.2, bf16[8,32,256]{2,1,0:T(8,128)(2,1)S(1)} %all_to_all.20.grad_ref, ...), custom_call_target="tpu_custom_call" | custom-call | flops 218000000 | bytes 1835008 | tf_op jit(solution)/shard_map/end/pallas_call | solution.py:35
Async XLA Ops:
  0.6 0.9 %copy-start.3 = (bf16[32,2048]{1,0:T(8,128)(2,1)S(1)}, bf16[32,2048]{1,0:T(8,128)(2,1)}, u32[]{:S(2)}) copy-start(bf16[32,2048]{1,0:T(8,128)(2,1)} %grad_ref.1) | copy-start | bytes 393220
  1.5 11.6 %copy-start.2 = (bf16[256,256]{1,0:T(8,128)(2,1)S(1)}, bf16[256,256]{1,0:T(8,128)(2,1)}, u32[]{:S(2)}) copy-start(bf16[256,256]{1,0:T(8,128)(2,1)} %value_ref.5) | copy-start | bytes 393220
  1.7 11.4 %copy-start = (bf16[256,256]{1,0:T(8,128)(2,1)S(1)}, bf16[256,256]{1,0:T(8,128)(2,1)}, u32[]{:S(2)}) copy-start(bf16[256,256]{1,0:T(8,128)(2,1)} %query_ref.5) | copy-start | bytes 393220
  1.7 11.4 %copy-start.1 = (bf16[256,256]{1,0:T(8,128)(2,1)S(1)}, bf16[256,256]{1,0:T(8,128)(2,1)}, u32[]{:S(2)}) copy-start(bf16[256,256]{1,0:T(8,128)(2,1)} %key_ref.5) | copy-start | bytes 393220

commit v8 on v7

--- a/solution.py
+++ b/solution.py
@@ -145,10 +145,11 @@
 
 
 def end_kernel(scale, query_ref, key_ref, value_ref, grad_ref, states_ref, *refs):
-    local_refs, out_refs = refs[:3], refs[3:]
+    local_refs, out_refs, (done_ref, sems) = refs[:3], refs[3:6], refs[6:]
     per_head = NEAR // 2
 
     def finish(locals_of):
+        copies = []
         grad = rows_of(grad_ref)
         for h in range(2):
             before, after = (
@@ -159,8 +160,15 @@
             )
             k, v, g = (r[:, head(h)] for r in (key_ref, value_ref, grad))
             far = (dot(g, before, 1, 1), dot(v, after, 1, 1), dot(k, after, 1, 0))
-            for total, local, out in zip(far, locals_of(h), out_refs):
-                out[:, head(h)] = ((total + local) * scale).astype(bf16)
+            for which, (total, local) in enumerate(zip(far, locals_of(h))):
+                done_ref[which, h] = ((total + local) * scale).astype(bf16)
+                copy = pltpu.make_async_copy(
+                    done_ref.at[which, h], out_refs[which].at[:, head(h)], sems.at[which, h]
+                )
+                copy.start()
+                copies.append(copy)
+        for copy in copies:
+            copy.wait()
 
     @pl.when(early())
     def _():
@@ -218,7 +226,9 @@
         grad,
         ends,
         *partial,
+        out_space=ANY,
         flops=218_000_000,
+        scratch=[pltpu.VMEM((3, 2, tokens, DH), bf16), pltpu.SemaphoreType.DMA((3, 2))],
     )
     return tuple(outs)
 

time: 57 us -> 57 us (level)
  no operation moved by 1% of the time
where the time goes in v8:
time: 57 us; the launch traced here: 56.7 us
  blocking collectives  53 us (93%)
  Pallas kernels  2.07 us (4%)
  local copies, waits for them, and re-layouts  0.91 us (2%)
  between operations  0.69 us (1%)
    all_to_all x1, blocking collectives, local(): lax.all_to_all(states, 'seq', 0, 0, axis_index_groups=NEAR_GROUPS, tiled=...  17.7 us
    all_to_all x1, blocking collectives, local(): lax.all_to_all(block, 'seq', 0, 0, axis_index_groups=FAR_GROUPS, tiled=True)  13.9 us
    all_to_all x1, blocking collectives, local(): lax.all_to_all(spread, 'head', 0, 0, axis_index_groups=[HEAD_ORDER], tile...  11.4 us
    all_to_all x1, blocking collectives, local(): lax.all_to_all(mine, 'seq', 0, 0, axis_index_groups=BACK_GROUPS, tiled=True)  10 us
    pallas_call x5, Pallas kernels, call(): pl.pallas_call(kernel, out_shape=[jax.ShapeDtypeStruct(shape, dtype) for...  2.07 us

profile of v8, /device:TPU:1, one launch (start us, length us, event | category | flops | bytes accessed | tf_op | source)
XLA Modules:
  0.0 56.7 jit_solution(10898190673873425593)
XLA Ops:
  0.6 0.0 copy-start.3
  0.6 0.9 %copy-done.3 = bf16[32,2048]{1,0:T(8,128)(2,1)S(1)} copy-done((bf16[32,2048]{1,0:T(8,128)(2,1)S(1)}, bf16[32,2048]{1,0:T(8,128)(2,1)}, u32[]{:S(2)}) %copy-start.3) | copy-done | bytes 131096
  1.5 0.0 copy-start.2
  1.5 0.1 spread.1
  1.7 0.0 copy-start
  1.7 0.0 copy-start.1
  1.7 11.4 %all_to_all.20.grad_ref = bf16[8,32,256]{2,1,0:T(8,128)(2,1)S(1)} all-to-all(bf16[8,32,256]{2,1,0:T(8,128)(2,1)S(1)} %spread.1), channel_id=1, replica_groups={{4,7,6,5,3,2,1,0},{12,15,14,13,11,10,9,8},{20,23,22,21,19,18,17,16},{28..., dimensions={0} | all-to-all | bytes 262144 | tf_op jit(solution)/shard_map/all_to_all | solution.py:197
  13.1 0.0 copy-done.2
  13.1 0.0 copy-done
  13.1 0.0 copy-done.1
  13.1 0.3 states.1
  13.4 17.7 %all_to_all.21.near_ref = bf16[8,2,32,128]{3,2,1,0:T(8,128)(2,1)S(1)} all-to-all(bf16[8,2,32,128]{3,2,1,0:T(8,128)(2,1)S(1)} %states.1), channel_id=1, replica_groups={{56,48,40,32,24,16,8,0},{120,112,104,96,88,80,72,64},{184,176,168,160,1..., dimensions={0} | all-to-all | bytes 262144 | tf_op jit(solution)/shard_map/all_to_all | solution.py:203
  31.1 0.6 %blocks.1 = (bf16[12,32,128]{2,1,0:T(8,128)(2,1)S(1)}, f32[256,256]{1,0:T(8,128)S(1)}, f32[256,256]{1,0:T(8,128)S(1)}, f32[256,256]{1,0:T(8,128)S(1)}) custom-call(bf16[8,2,32,128]{3,2,1,0:T(8,128)(2,1)S(1)} %all_to_all.21.near_ref, bf16[256,256]{1,0:T(8,128)(2,1)S(1)} %copy-done, bf16[256,256]{1,0:T(8,128)(2,1)S(1)} %copy-done.1, ...), custom_call_target="tpu_custom_call" | custom-call | flops 168000000 | bytes 1540096 | tf_op jit(solution)/shard_map/blocks/pallas_call | solution.py:35
  31.7 13.9 %all_to_all.22.far_ref = bf16[12,32,128]{2,1,0:T(8,128)(2,1)S(1)} all-to-all(bf16[12,32,128]{2,1,0:T(8,128)(2,1)S(1)} %get-tuple-element.7), channel_id=1, replica_groups={{512,704,640,576,448,384,320,256,192,128,64,0},{520,712,648,584,456,392..., dimensions={0} | all-to-all | bytes 196608 | tf_op jit(solution)/shard_map/all_to_all | solution.py:216
  45.6 0.1 prefix.1
  45.7 10.0 %all_to_all.23.states_ref = bf16[8,2,32,128]{3,2,1,0:T(8,128)(2,1)S(1)} all-to-all(bf16[8,2,32,128]{3,2,1,0:T(8,128)(2,1)S(1)} %prefix.1), channel_id=1, replica_groups={{40,56,48,32,24,16,8,0},{104,120,112,96,88,80,72,64},{168,184,176,160,1..., dimensions={0} | all-to-all | bytes 262144 | tf_op jit(solution)/shard_map/all_to_all | solution.py:218
  55.7 1.0 %end.1 = (bf16[256,256]{1,0:T(8,128)(2,1)}, bf16[256,256]{1,0:T(8,128)(2,1)}, bf16[256,256]{1,0:T(8,128)(2,1)}) custom-call(bf16[256,256]{1,0:T(8,128)(2,1)S(1)} %copy-done, bf16[256,256]{1,0:T(8,128)(2,1)S(1)} %copy-done.1, bf16[256,256]{1,0:T(8,128)(2,1)S(1)} %copy-done.2, bf16[8,32,256]{2,1,0:T(8,128)(2,1)S(1)} %all_to_all.20.grad_ref, ...), custom_call_target="tpu_custom_call" | custom-call | flops 218000000 | bytes 1835008 | tf_op jit(solution)/shard_map/end/pallas_call | solution.py:35
Async XLA Ops:
  0.6 0.9 %copy-start.3 = (bf16[32,2048]{1,0:T(8,128)(2,1)S(1)}, bf16[32,2048]{1,0:T(8,128)(2,1)}, u32[]{:S(2)}) copy-start(bf16[32,2048]{1,0:T(8,128)(2,1)} %grad_ref.1) | copy-start | bytes 393220
  1.5 11.6 %copy-start.2 = (bf16[256,256]{1,0:T(8,128)(2,1)S(1)}, bf16[256,256]{1,0:T(8,128)(2,1)}, u32[]{:S(2)}) copy-start(bf16[256,256]{1,0:T(8,128)(2,1)} %value_ref.5) | copy-start | bytes 393220
  1.7 11.4 %copy-start = (bf16[256,256]{1,0:T(8,128)(2,1)S(1)}, bf16[256,256]{1,0:T(8,128)(2,1)}, u32[]{:S(2)}) copy-start(bf16[256,256]{1,0:T(8,128)(2,1)} %query_ref.5) | copy-start | bytes 393220
  1.7 11.4 %copy-start.1 = (bf16[256,256]{1,0:T(8,128)(2,1)S(1)}, bf16[256,256]{1,0:T(8,128)(2,1)}, u32[]{:S(2)}) copy-start(bf16[256,256]{1,0:T(8,128)(2,1)} %key_ref.5) | copy-start | bytes 393220
